TPU v7x, 512 devices: a whole 4x4x16 slice. The times are simulated.
512 devices in a mesh: fsdp: 128 (over x, z_hi, y, core), seq: 4 (over z_lo).
Axes of the slice: x: 4, y: 4, z: 16 (z_hi: 4, z_lo: 4; z = z_hi * 4 + z_lo), core: 2. Of those that a mesh axis runs over, the one named last changes fastest.
Arguments:
- query_frames: bfloat16 [16, 4096, 2048], P('seq', 'fsdp'), may hold values from -6 to 6
- key_frames: bfloat16 [16, 4096, 2048], P('seq', 'fsdp'), may hold values from -6 to 6
- value_frames: bfloat16 [16, 4096, 2048], P('seq', 'fsdp'), may hold values from -24 to 24
- out_weight: bfloat16 [2048, 2048], P('fsdp', 'seq'), may hold values from -0.125 to 0.125
- out_grad: bfloat16 [16, 4096, 2048], P(None, 'fsdp', 'seq'), may hold values from -1.5 to 1.5
Outputs:
- block_out: bfloat16 [16, 4096, 2048], P(None, 'fsdp', 'seq')
- query_grad: bfloat16 [16, 4096, 2048], P('seq', 'fsdp')
- key_grad: bfloat16 [16, 4096, 2048], P('seq', 'fsdp')
- value_grad: bfloat16 [16, 4096, 2048], P('seq', 'fsdp')
- weight_grad: float32 [2048, 2048], P('fsdp', 'seq')
All inputs are finite; a program needn't handle non-finite values.
Results may differ from a plain program's by a relative error of at most 0.0058.
Values may be sent and summed in bfloat16 or wider, within the bound.
No kernel may reach another device: no remote copies, remote signals or barrier semaphores. Data moves between devices by JAX's collectives and lax.ppermute only.
A program may use at most 64 MiB of HBM per device.

v0:
```python
import math

import jax
import jax.numpy as jnp
from jax import lax
from jax.sharding import PartitionSpec as P

HD = 128


def split_heads(array):
    return array.reshape(array.shape[0], array.shape[1], -1, HD)


def join_heads(array):
    return array.reshape(array.shape[0], array.shape[1], -1)


def causal_weights(query_heads, key_heads):
    frames = query_heads.shape[0]
    scores = jnp.einsum(
        "tphd,sphd->phts", query_heads, key_heads, preferred_element_type=jnp.float32
    ) * (1.0 / math.sqrt(HD))
    allowed = lax.broadcasted_iota(jnp.int32, (frames, frames), 0) >= lax.broadcasted_iota(
        jnp.int32, (frames, frames), 1
    )
    scores = jnp.where(allowed, scores, -1e30)
    peak_score = jnp.max(scores, axis=-1, keepdims=True)
    expo_terms = jnp.exp(scores - peak_score)
    return expo_terms / jnp.sum(expo_terms, axis=-1, keepdims=True)


def per_device(query_frames, key_frames, value_frames, out_weight, out_grad):
    query_local, key_local, value_local = (
        lax.all_to_all(query_frames, "seq", split_axis=2, concat_axis=0, tiled=True),
        lax.all_to_all(key_frames, "seq", split_axis=2, concat_axis=0, tiled=True),
        lax.all_to_all(value_frames, "seq", split_axis=2, concat_axis=0, tiled=True),
    )
    query_heads = split_heads(query_local)
    key_heads = split_heads(key_local)
    value_heads = split_heads(value_local)
    weights = causal_weights(query_heads, key_heads)
    weights_b = weights.astype(jnp.bfloat16)
    attended = join_heads(
        jnp.einsum(
            "phts,sphd->tphd", weights_b, value_heads, preferred_element_type=jnp.float32
        ).astype(jnp.bfloat16)
    )
    attended_all = lax.all_gather(attended, "seq", axis=2, tiled=True)
    weight_panel = lax.all_gather(out_weight, "fsdp", axis=0, tiled=True)
    out_sum = jnp.einsum(
        "tpc,cd->tpd", attended_all, weight_panel, preferred_element_type=jnp.float32
    )
    block_out = out_sum.astype(jnp.bfloat16)
    grad_all = lax.all_gather(out_grad, "seq", axis=2, tiled=True)
    head_weight = lax.all_to_all(weight_panel, "seq", split_axis=0, concat_axis=1, tiled=True)
    attended_grad = jnp.einsum(
        "tpd,cd->tpc", grad_all, head_weight, preferred_element_type=jnp.float32
    ).astype(jnp.bfloat16)
    weight_grad = lax.psum_scatter(
        jnp.einsum("tpc,tpd->cd", attended_all, out_grad, preferred_element_type=jnp.float32),
        "fsdp",
        scatter_dimension=0,
        tiled=True,
    )
    grad_heads = split_heads(attended_grad)
    value_grad = join_heads(
        jnp.einsum(
            "phts,tphd->sphd", weights_b, grad_heads, preferred_element_type=jnp.float32
        ).astype(jnp.bfloat16)
    )
    weights_grad = jnp.einsum(
        "tphd,sphd->phts", grad_heads, value_heads, preferred_element_type=jnp.float32
    )
    scores_grad = weights * (weights_grad - jnp.sum(weights * weights_grad, axis=-1, keepdims=True))
    scaled_b = (scores_grad * (1.0 / math.sqrt(HD))).astype(jnp.bfloat16)
    query_grad = join_heads(
        jnp.einsum(
            "phts,sphd->tphd", scaled_b, key_heads, preferred_element_type=jnp.float32
        ).astype(jnp.bfloat16)
    )
    key_grad = join_heads(
        jnp.einsum(
            "phts,tphd->sphd", scaled_b, query_heads, preferred_element_type=jnp.float32
        ).astype(jnp.bfloat16)
    )
    query_back, key_back, value_back = (
        lax.all_to_all(query_grad, "seq", split_axis=0, concat_axis=2, tiled=True),
        lax.all_to_all(key_grad, "seq", split_axis=0, concat_axis=2, tiled=True),
        lax.all_to_all(value_grad, "seq", split_axis=0, concat_axis=2, tiled=True),
    )
    return (block_out, query_back, key_back, value_back, weight_grad)


def solution(mesh):
    return jax.shard_map(
        per_device,
        mesh=mesh,
        in_specs=(
            P("seq", "fsdp", None),
            P("seq", "fsdp", None),
            P("seq", "fsdp", None),
            P("fsdp", "seq"),
            P(None, "fsdp", "seq"),
        ),
        out_specs=(
            P(None, "fsdp", "seq"),
            P("seq", "fsdp", None),
            P("seq", "fsdp", None),
            P("seq", "fsdp", None),
            P("fsdp", "seq"),
        ),
        check_vma=False,
    )
```

profile of v0, /device:TPU:32, one launch (start us, length us, event | category | flops | bytes accessed | tf_op | source)
XLA Modules:
  0.0 1117.0 jit_solution(1045292386056926200)
XLA Ops:
  10.0 2.9 reshape.59
  12.9 8.9 all-to-all-start
  24.0 2.9 reshape.57
  26.9 3.6 all-to-all-done
  30.6 6.3 all-to-all-start.1
  39.7 2.9 reshape.55
  42.6 3.6 all-to-all-done.1
  46.2 7.1 all-to-all-start.2
  71.1 61.8 %all-gather.6.cloned.1.call-done = bf16[2048,512]{1,0:T(8,128)(2,1)} async-done(((bf16[16,512]{1,0:T(8,128)(2,1)}), bf16[2048,512]{1,0:T(8,128)(2,1)}) %all-gather.6.cloned.1.call-update) | async-done | bytes 2097168 | tf_op jit(solution)/shard_map/all_gather | solution.py:50
  133.0 5.1 all-to-all-start.3
  139.0 79.5 %all-gather.4.cloned.1.call-done = bf16[16,32,2048]{2,1,0:T(8,128)(2,1)} async-done(((bf16[16,32,512]{2,1,0:T(8,128)(2,1)}), bf16[16,32,2048]{2,1,0:T(8,128)(2,1)}) %all-gather.4.cloned.1.call-update) | async-done | bytes 2097168 | tf_op jit(solution)/shard_map/all_gather | solution.py:49
  218.6 4.8 convolution_bitcast_fusion
  223.4 2.9 copy.65
  226.4 3.3 reshape.52
  229.6 42.7 %all-gather.8.cloned.1.call-done = bf16[16,32,2048]{2,1,0:T(8,128)(2,1)} async-done(((bf16[16,32,512]{2,1,0:T(8,128)(2,1)}), bf16[16,32,2048]{2,1,0:T(8,128)(2,1)}) %all-gather.8.cloned.1.call-update) | async-done | bytes 2097168 | tf_op jit(solution)/shard_map/all_gather | solution.py:55
  278.3 4.9 all-to-all-start.6
  287.6 6.9 all-to-all-done.6
  294.5 7.0 all-to-all-start.4
  301.5 3.1 fusion.16
  308.9 4.6 all-to-all-done.4
  313.5 7.5 all-to-all-start.5
  321.0 3.6 fusion.10
  326.3 6.3 all-to-all-done.5
  334.6 776.0 %reduce-scatter.2.cloned.1.call-done = f32[16,512]{1,0:T(8,128)} async-done(((f32[2048,512]{1,0:T(8,128)}), f32[16,512]{1,0:T(8,128)}) %reduce-scatter.2.cloned.1.call-update) | async-done | bytes 32784 | tf_op jit(solution)/shard_map/reduce_scatter | solution.py:60
  (53 shorter events, 44.7 us)
Async XLA Ops:
  10.0 12.6 %copy-start.1 = (bf16[4,32,2048]{2,1,0:T(8,128)(2,1)S(1)}, bf16[4,32,2048]{2,1,0:T(8,128)(2,1)}, u32[]{:S(2)}) copy-start(bf16[4,32,2048]{2,1,0:T(8,128)(2,1)} %param.6) | copy-start | bytes 1572868
  12.9 17.6 %all-to-all-start = ((bf16[4,2,32768]{2,1,0:T(2,128)(2,1)}), bf16[4,2,32768]{2,1,0:T(2,128)(2,1)S(1)}, u32[]{:S(2)}, u32[]{:S(2)}) async-start(bf16[4,2,32768]{2,1,0:T(2,128)(2,1)} %reshape.59), calls=%async_computation | async-start | bytes 1048576 | tf_op jit(solution)/shard_map/all_to_all | solution.py:35
  21.9 111.1 %all-gather.6.cloned.1.call-start = ((), (), s32[]{:S(2)}) async-start(), calls=%async_computation.9 | async-start | bytes 2113536 | tf_op jit(solution)/shard_map/all_gather | solution.py:50
  30.6 15.6 %all-to-all-start.1 = ((bf16[4,2,32768]{2,1,0:T(2,128)(2,1)}), bf16[4,2,32768]{2,1,0:T(2,128)(2,1)S(1)}, u32[]{:S(2)}, u32[]{:S(2)}) async-start(bf16[4,2,32768]{2,1,0:T(2,128)(2,1)} %reshape.57), calls=%async_computation.1 | async-start | bytes 1048576 | tf_op jit(solution)/shard_map/all_to_all | solution.py:36
  46.2 16.2 %all-to-all-start.2 = ((bf16[4,2,32768]{2,1,0:T(2,128)(2,1)}), bf16[4,2,32768]{2,1,0:T(2,128)(2,1)}, u32[]{:S(2)}, u32[]{:S(2)}) async-start(bf16[4,2,32768]{2,1,0:T(2,128)(2,1)} %reshape.55), calls=%async_computation.2 | async-start | bytes 1048576 | tf_op jit(solution)/shard_map/all_to_all | solution.py:37
  53.2 165.3 %all-gather.4.cloned.1.call-start = ((), (), s32[]{:S(2)}) async-start(), calls=%async_computation.8 | async-start | bytes 2621440 | tf_op jit(solution)/shard_map/all_gather | solution.py:49
  68.8 1.0 copy-start.5
  133.0 85.6 %copy-start.2 = (bf16[16,32,512]{2,1,0:T(8,128)(2,1)S(1)}, bf16[16,32,512]{2,1,0:T(8,128)(2,1)}, u32[]{:S(2)}) copy-start(bf16[16,32,512]{2,1,0:T(8,128)(2,1)} %param.9) | copy-start | bytes 1572868
  133.0 90.4 %all-to-all-start.3 = ((bf16[4,512,512]{2,1,0:T(8,128)(2,1)}), bf16[4,512,512]{2,1,0:T(8,128)(2,1)S(1)}, u32[]{:S(2)}, u32[]{:S(2)}) async-start(bf16[4,512,512]{2,1,0:T(8,128)(2,1)} %bitcast.65), calls=%async_computation.3 | async-start | bytes 4194304 | tf_op jit(solution)/shard_map/all_to_all | solution.py:56
  138.1 134.2 %all-gather.8.cloned.1.call-start = ((), (), s32[]{:S(2)}) async-start(), calls=%async_computation.10 | async-start | bytes 2621440 | tf_op jit(solution)/shard_map/all_gather | solution.py:55
  138.8 971.7 %reduce-scatter.2.cloned.1.call-start = ((), (), s32[]{:S(2)}) async-start(), calls=%async_computation.11 | async-start | bytes 4227072 | tf_op jit(solution)/shard_map/reduce_scatter | solution.py:60
  277.3 6.6 copy-start.4
  278.3 16.2 %all-to-all-start.6 = ((bf16[16,32,512]{2,1,0:T(8,128)(2,1)}), bf16[16,32,512]{2,1,0:T(8,128)(2,1)S(1)}, u32[]{:S(2)}, u32[]{:S(2)}) async-start(bf16[16,32,512]{2,1,0:T(8,128)(2,1)} %reshape.50), calls=%async_computation.6 | async-start | bytes 1048576 | tf_op jit(solution)/shard_map/all_to_all | solution.py:90
  286.3 15.2 %copy-start.3 = (bf16[16,32,4,128]{3,2,1,0:T(4,128)(2,1)S(1)}, bf16[16,32,4,128]{3,2,1,0:T(4,128)(2,1)}, u32[]{:S(2)}) copy-start(bf16[16,32,4,128]{3,2,1,0:T(4,128)(2,1)} %reshape.43) | copy-start | bytes 1572868
  294.5 19.0 %all-to-all-start.4 = ((bf16[16,32,512]{2,1,0:T(8,128)(2,1)}), bf16[16,32,512]{2,1,0:T(8,128)(2,1)S(1)}, u32[]{:S(2)}, u32[]{:S(2)}) async-start(bf16[16,32,512]{2,1,0:T(8,128)(2,1)} %reshape.48), calls=%async_computation.4 | async-start | bytes 1048576 | tf_op jit(solution)/shard_map/all_to_all | solution.py:88
  304.6 16.4 %copy-start = (bf16[2048,512]{1,0:T(8,128)(2,1)S(1)}, bf16[2048,512]{1,0:T(8,128)(2,1)}, u32[]{:S(2)}) copy-start(bf16[2048,512]{1,0:T(8,128)(2,1)} %all-gather.6.cloned.1.call-done) | copy-start | bytes 6291460
  313.5 19.2 %all-to-all-start.5 = ((bf16[16,32,512]{2,1,0:T(8,128)(2,1)}), bf16[16,32,512]{2,1,0:T(8,128)(2,1)}, u32[]{:S(2)}, u32[]{:S(2)}) async-start(bf16[16,32,512]{2,1,0:T(8,128)(2,1)} %reshape.49), calls=%async_computation.5 | async-start | bytes 1048576 | tf_op jit(solution)/shard_map/all_to_all | solution.py:89
Sparse Core Ops, SparseCore 0:
  27.1 105.7 all-gather.5
  135.6 82.8 all-gather.3
  220.7 51.6 all-gather.7
  275.5 834.9 reduce-scatter.1
where the time goes:
time: 1120 us
  waiting for transfers between devices  989 us (88%)
  starting transfers between devices  47 us (4%)
  local copies, waits for them, and re-layouts  44.8 us (4%)
  matrix products  22.1 us (2%)
  between operations  14 us (1%)
    reduce_scatter x1, waiting for transfers between devices, per_device(): lax.psum_scatter(jnp.einsum('tpc,tpd->cd', attended_all, out_grad, prefer...  776 us
    all_gather x1, waiting for transfers between devices, per_device(): attended_all = lax.all_gather(attended, 'seq', axis=2, tiled=True)  79.5 us
    all_gather x1, waiting for transfers between devices, per_device(): weight_panel = lax.all_gather(out_weight, 'fsdp', axis=0, tiled=True)  61.8 us
    all_gather x1, waiting for transfers between devices, per_device(): grad_all = lax.all_gather(out_grad, 'seq', axis=2, tiled=True)  42.7 us
  transfers between devices with their start and end apart: 11, of which 10 were waited for; matrix products, arithmetic and copies ran while one was open for 5% of the time, Pallas kernels for 0%

commit v1 on v0

v1 whole, which is shorter than its diff:
```python
import functools
import math

import jax
import jax.numpy as jnp
from jax import lax
from jax.experimental import pallas as pl
from jax.experimental.pallas import tpu as pltpu
from jax.sharding import Mesh
from jax.sharding import PartitionSpec as P

HD = 128
SCALE = 1.0 / math.sqrt(HD)
BF = jnp.bfloat16
F32 = jnp.float32
VMEM = pl.BlockSpec(memory_space=pltpu.VMEM)
SMEM = pl.BlockSpec(memory_space=pltpu.SMEM)
ANY = pl.BlockSpec(memory_space=pl.ANY)
NT = (((1,), (1,)), ((), ()))
TN = (((0,), (0,)), ((), ()))
NN = (((1,), (0,)), ((), ()))
X, ZH, Y, C, S = range(5)
DEVICES = ("x", "zh", "y", "c", "s")


def dot(a, b, dims):
    return lax.dot_general(a, b, dims, preferred_element_type=F32)


def shift(array, axis, step):
    return lax.ppermute(array, axis, [(i, (i + step) % 4) for i in range(4)])


def params(mib):
    return pltpu.CompilerParams(vmem_limit_bytes=mib * 2**20)


def wrap(index, step):
    return lax.rem(index + step, 4)


def run_copies(pairs, sems):
    copies = [pltpu.make_async_copy(src, dst, sems.at[n]) for n, (src, dst) in enumerate(pairs)]
    for copy in copies:
        copy.start()
    return copies


def wait_all(copies):
    for copy in copies:
        copy.wait()


def pack_kernel(pos_ref, q_ref, k_ref, v_ref, g_ref, o0, o1, o2, o3, rows_ref, grad_ref, wide_ref, sems):
    pairs = [(ref, rows_ref.at[which]) for which, ref in enumerate((q_ref, k_ref, v_ref))]
    copies = run_copies(pairs + [(g_ref, grad_ref)], sems)
    for which in range(4):
        copies[which].wait()
        for part in range(4):
            lanes = slice(512 * part, 512 * part + 512)
            block = rows_ref[which, :, :, lanes] if which < 3 else grad_ref[4 * part : 4 * part + 4]
            wide_ref[part] = block.astype(F32)
            for step, out in enumerate((o0, o1, o2, o3)):
                pixels = pl.ds(pl.multiple_of(wrap(pos_ref[S], step) * 8, 8), 8)
                out[which, :, lanes] = wide_ref[part, :, pixels, :].reshape(32, 512).astype(BF)


def unpack_kernel(pos_ref, h0, h1, h2, h3, q_ref, k_ref, v_ref, rows_ref, wide_ref, sems):
    copies = run_copies([(ref, rows_ref.at[step]) for step, ref in enumerate((h0, h1, h2, h3))], sems)
    wait_all(copies)
    for which, out in enumerate((q_ref, k_ref, v_ref)):
        for part in range(4):
            lanes = slice(512 * part, 512 * part + 512)
            for step in range(4):
                pixels = pl.ds(pl.multiple_of(wrap(pos_ref[S], 4 - step) * 8, 8), 8)
                wide_ref[part, :, pixels, :] = rows_ref[step, which, :, lanes].astype(F32).reshape(4, 8, 512)
            out[:, :, lanes] = wide_ref[part].astype(BF)


def allowed_pairs():
    row = lax.broadcasted_iota(jnp.int32, (128, 128), 0)
    col = lax.broadcasted_iota(jnp.int32, (128, 128), 1)
    return ((row & 7) == (col & 7)) & (col <= row)


def softmax_heads(qs, ks, allowed):
    scores = [jnp.where(allowed, dot(q, k, NT) * SCALE, -1e30) for q, k in zip(qs, ks)]
    peaks = [jnp.max(s, axis=-1, keepdims=True) for s in scores]
    terms = [jnp.exp(s - p) for s, p in zip(scores, peaks)]
    sums = [jnp.sum(t, axis=-1, keepdims=True) for t in terms]
    return [t / s for t, s in zip(terms, sums)]


def heads_of(all_ref, which, heads):
    return [all_ref[which, :, :, 128 * h : 128 * h + 128].reshape(128, 128) for h in heads]


def inputs_of(pos_ref, pieces, all_ref):
    return [(ref.at[0:3], all_ref.at[:, wrap(pos_ref[S], 4 - step)]) for step, ref in enumerate(pieces)]


def forward_kernel(pos_ref, e0, e1, e2, e3, att_ref, all_ref, sems):
    wait_all(run_copies(inputs_of(pos_ref, (e0, e1, e2, e3), all_ref), sems))
    allowed = allowed_pairs()
    for block in range(4):
        heads = [4 * block + i for i in range(4)]
        qs, ks, vs = (heads_of(all_ref, which, heads) for which in range(3))
        weights = softmax_heads(qs, ks, allowed)
        for h, w, v in zip(heads, weights, vs):
            att_ref[:, 128 * h : 128 * h + 128] = dot(w.astype(BF), v, NN).astype(BF)


def backward_kernel(
    pos_ref, e0, e1, e2, e3, mine_ref, other_ref, f0, f1, f2, f3, w_ref, all_ref, grad_ref, ag_ref, sems, out_sems
):
    pieces = (e0, e1, e2, e3)
    pairs = []
    for core, ref in enumerate((mine_ref, other_ref)):
        c = pos_ref[C] if core == 0 else 1 - pos_ref[C]
        pairs += [(ref.at[:, :, s, zh], w_ref.at[s, :, zh, :, c]) for s in range(4) for zh in range(4)]
    for step, ref in enumerate(pieces):
        lanes = pl.ds(pl.multiple_of(wrap(pos_ref[S], 4 - step) * 512, 512), 512)
        pairs += [(ref.at[3, :, 512 * g : 512 * g + 512], grad_ref.at[g, :, lanes]) for g in range(4)]
    pairs += inputs_of(pos_ref, pieces, all_ref)
    wait_all(run_copies(pairs, sems))
    total = None
    for s in range(4):
        rows = grad_ref[:, :, 512 * s : 512 * s + 512].reshape(128, 512)
        part = dot(rows, w_ref[s].reshape(2048, 512), NT)
        total = part if total is None else total + part
    ag_ref[...] = total.astype(BF)
    allowed = allowed_pairs()
    for block in range(4):
        heads = [4 * block + i for i in range(4)]
        qs, ks, vs = (heads_of(all_ref, which, heads) for which in range(3))
        gs = [ag_ref[:, 128 * h : 128 * h + 128] for h in heads]
        weights = softmax_heads(qs, ks, allowed)
        wgrads = [dot(g, v, NT) for g, v in zip(gs, vs)]
        dvs = [dot(w.astype(BF), g, TN) for w, g in zip(weights, gs)]
        means = [jnp.sum(w * d, axis=-1, keepdims=True) for w, d in zip(weights, wgrads)]
        sgrads = [(w * (d - m) * SCALE).astype(BF) for w, d, m in zip(weights, wgrads, means)]
        dqs = [dot(d, k, NN) for d, k in zip(sgrads, ks)]
        dks = [dot(d, q, TN) for d, q in zip(sgrads, qs)]
        for which, grads in enumerate((dqs, dks, dvs)):
            for h, grad in zip(heads, grads):
                all_ref[which, :, :, 128 * h : 128 * h + 128] = grad.astype(BF).reshape(4, 32, 128)
    pairs = [(all_ref.at[:, wrap(pos_ref[S], step)], out) for step, out in enumerate((f0, f1, f2, f3))]
    wait_all(run_copies(pairs, out_sems))


def weight_kernel(pos_ref, a0, a1, a2, a3, p0, p1, p2, p3, keep_ref, send_ref, att_ref, grad_ref, sum_ref, sems):
    pairs = [(ref, att_ref.at[step]) for step, ref in enumerate((a0, a1, a2, a3))]
    for step, ref in enumerate((p0, p3, p2, p1)):
        pairs += [(ref.at[3, :, 512 * g : 512 * g + 512], grad_ref.at[step, g]) for g in range(4)]
    wait_all(run_copies(pairs, sems))
    grads = grad_ref[...].reshape(512, 512)
    c = pos_ref[C]
    for block in range(4):
        att = att_ref[:, :, 512 * block : 512 * block + 512].reshape(512, 512)
        sum_ref[...] = dot(att, grads, TN).reshape(4, 4, 2, 16, 512)
        for zh in range(4):
            keep_ref[block, :, zh] = sum_ref[zh, :, c]
            send_ref[block, :, zh] = sum_ref[zh, :, 1 - c]


def output_kernel(pos_ref, a0, a1, a2, a3, mine_ref, other_ref, out_ref, w_ref, att_ref, wide_ref, sems):
    pairs = [(ref, att_ref.at[step]) for step, ref in enumerate((a0, a1, a2, a3))]
    for core, ref in enumerate((mine_ref, other_ref)):
        c = pos_ref[C] if core == 0 else 1 - pos_ref[C]
        pairs += [(ref.at[:, :, pos_ref[S], zh], w_ref.at[:, zh, :, c]) for zh in range(4)]
    wait_all(run_copies(pairs, sems))
    rows = dot(att_ref[...].reshape(512, 2048), w_ref[...].reshape(2048, 512), NN).reshape(4, 16, 8, 512)
    for step in range(4):
        pixels = pl.ds(pl.multiple_of(wrap(pos_ref[S], 4 - step) * 8, 8), 8)
        wide_ref[:, pixels, :] = rows[step]
    out_ref[...] = wide_ref[...].astype(BF)


def call(kernel, name, out_shape, inputs, out_spec, scratch, mib):
    return pl.pallas_call(
        kernel,
        out_shape=out_shape,
        in_specs=[SMEM] + [ANY] * (len(inputs) - 1),
        out_specs=jax.tree.map(lambda _: out_spec, out_shape),
        scratch_shapes=scratch,
        compiler_params=params(mib),
        name=name,
    )(*inputs)


def per_device(query_frames, key_frames, value_frames, out_weight, out_grad):
    pos = jnp.stack([lax.axis_index(a) for a in DEVICES]).astype(jnp.int32)
    swap = [(0, 1), (1, 0)]
    dma = pltpu.SemaphoreType.DMA

    spread = jnp.broadcast_to(out_weight[None], (16, 16, 512))
    column = lax.all_to_all(spread, ("s", "zh"), 0, 0)

    parcel = jax.ShapeDtypeStruct((4, 32, 2048), BF)
    sent = call(
        pack_kernel, "pack", [parcel] * 4, (pos, query_frames, key_frames, value_frames, out_grad), VMEM,
        [pltpu.VMEM((3, 4, 32, 2048), BF), pltpu.VMEM((16, 32, 512), BF), pltpu.VMEM((4, 4, 32, 512), F32), dma((4,))], 32,
    )
    column, sent = lax.optimization_barrier((column, sent))
    arrived = [sent[0]] + [shift(sent[n], "s", n) for n in (1, 2, 3)]
    mine = lax.all_gather(column.reshape(256, 512), ("x", "y"), axis=0, tiled=True).reshape(4, 4, 4, 4, 16, 512)

    attended = call(
        forward_kernel, "forward", jax.ShapeDtypeStruct((128, 2048), BF), (pos, *arrived), VMEM,
        [pltpu.VMEM((3, 4, 32, 2048), BF), dma((4,))], 24,
    )
    attended_all = [attended] + [shift(attended, "s", n) for n in (1, 2, 3)]
    mine, attended_all[1] = lax.optimization_barrier((mine, attended_all[1]))
    other = lax.ppermute(mine, "c", swap)

    back = call(
        backward_kernel, "backward", [jax.ShapeDtypeStruct((3, 32, 2048), BF)] * 4, (pos, *arrived, mine, other), ANY,
        [
            pltpu.VMEM((4, 4, 4, 4, 2, 16, 512), BF),
            pltpu.VMEM((3, 4, 32, 2048), BF),
            pltpu.VMEM((4, 32, 2048), BF),
            pltpu.VMEM((128, 2048), BF),
            dma((52,)),
            dma((4,)),
        ],
        40,
    )
    home = [back[0]] + [shift(back[n], "s", n) for n in (1, 2, 3)]

    home[1], *attended_all = lax.optimization_barrier((home[1], *attended_all))
    quarter = jax.ShapeDtypeStruct((4, 4, 4, 16, 512), F32)
    keep, send = call(
        weight_kernel, "weight", [quarter] * 2, (pos, *attended_all, *sent), VMEM,
        [
            pltpu.VMEM((4, 128, 2048), BF),
            pltpu.VMEM((4, 4, 32, 512), BF),
            pltpu.VMEM((4, 4, 2, 16, 512), F32),
            dma((20,)),
        ],
        32,
    )
    chip_sum = keep + lax.ppermute(send, "c", swap)
    parts = lax.all_to_all(chip_sum.reshape(16, 4, 16, 512), ("x", "y"), 0, 0)

    block_out = call(
        output_kernel, "project", jax.ShapeDtypeStruct((16, 32, 512), BF), (pos, *attended_all, mine, other), VMEM,
        [
            pltpu.VMEM((4, 4, 4, 2, 16, 512), BF),
            pltpu.VMEM((4, 128, 2048), BF),
            pltpu.VMEM((16, 32, 512), F32),
            dma((12,)),
        ],
        32,
    )
    query_grad, key_grad, value_grad = call(
        unpack_kernel, "unpack", [jax.ShapeDtypeStruct((4, 32, 2048), BF)] * 3, (pos, *home), VMEM,
        [pltpu.VMEM((4, 3, 32, 2048), BF), pltpu.VMEM((4, 4, 32, 512), F32), dma((4,))], 32,
    )
    parts, block_out, query_grad, key_grad, value_grad = lax.optimization_barrier(
        (parts, block_out, query_grad, key_grad, value_grad)
    )
    plane_sum = parts.sum(axis=0)
    weight_grad = None
    for step in range(4):
        part = lax.dynamic_index_in_dim(plane_sum, wrap(pos[ZH], step), 0, keepdims=False)
        got = part if step == 0 else shift(part, "zh", step)
        weight_grad = got if weight_grad is None else weight_grad + got
    return block_out, query_grad, key_grad, value_grad, weight_grad


def solution(mesh):
    fine = Mesh(mesh.devices.reshape(4, 4, 4, 2, 4), ("x", "zh", "y", "c", "s"))
    fsdp = ("x", "zh", "y", "c")
    return jax.shard_map(
        per_device,
        mesh=fine,
        in_specs=(
            P("s", fsdp, None),
            P("s", fsdp, None),
            P("s", fsdp, None),
            P(fsdp, "s"),
            P(None, fsdp, "s"),
        ),
        out_specs=(
            P(None, fsdp, "s"),
            P("s", fsdp, None),
            P("s", fsdp, None),
            P("s", fsdp, None),
            P(fsdp, "s"),
        ),
        check_vma=False,
    )
```

time: 1120 us -> 244 us (0.22)
  the two profiles are of different devices: /device:TPU:32 before, /device:TPU:2 now
where the time goes in v1:
time: 244 us; the launch traced here: 243 us
  starting transfers between devices  97.8 us (40%)
  waiting for transfers between devices  88.5 us (36%)
  Pallas kernels  20.6 us (8%)
  local copies, waits for them, and re-layouts  17.5 us (7%)
  between operations  14.4 us (6%)
  other arithmetic  4.44 us (2%)
    ppermute x12, waiting for transfers between devices, shift(): return lax.ppermute(array, axis, [(i, (i + step) % 4) for i in range(4)])  72.5 us
    ppermute x12, starting transfers between devices, shift(): return lax.ppermute(array, axis, [(i, (i + step) % 4) for i in range(4)])  71.3 us
    pallas_call x6, Pallas kernels, call(): pl.pallas_call(kernel, out_shape=out_shape, in_specs=[SMEM] + [ANY] * (le...  20.6 us
    unnamed x42, local copies, waits for them, and re-layouts  16 us
    all_to_all x1, starting transfers between devices, per_device(): column = lax.all_to_all(spread, ('s', 'zh'), 0, 0)  15.2 us
    all_to_all x1, waiting for transfers between devices, per_device(): column = lax.all_to_all(spread, ('s', 'zh'), 0, 0)  11.8 us
    all_to_all x1, starting transfers between devices, per_device(): parts = lax.all_to_all(chip_sum.reshape(16, 4, 16, 512), ('x', 'y'), 0, 0)  7.48 us
  transfers between devices with their start and end apart: 17, of which 12 were waited for; matrix products, arithmetic and copies ran while one was open for 0% of the time, Pallas kernels for 7%

profile of v1, /device:TPU:2, one launch (start us, length us, event | category | flops | bytes accessed | tf_op | source)
XLA Modules:
  0.0 243.2 jit_solution(7697233552414519470)
XLA Ops:
  8.6 15.2 %all-to-all-start = ((bf16[16,16,512]{2,1,0:T(8,128)(2,1)}), bf16[16,16,512]{2,1,0:T(8,128)(2,1)S(1)}, u32[]{:S(2)}, u32[]{:S(2)}) async-start(bf16[16,16,512]{2,1,0:T(8,128)(2,1)} %broadcast_in_dim.2), calls=%async_computation | async-start | bytes 524288 | tf_op jit(solution)/shard_map/all_to_all | solution.py:197
  29.5 11.8 %all-to-all-done = bf16[16,16,512]{2,1,0:T(8,128)(2,1)S(1)} async-done(((bf16[16,16,512]{2,1,0:T(8,128)(2,1)}), bf16[16,16,512]{2,1,0:T(8,128)(2,1)S(1)}, u32[]{:S(2)}, u32[]{:S(2)}) %all-to-all-start) | async-done | bytes 262176 | tf_op jit(solution)/shard_map/all_to_all | solution.py:197
  42.1 6.1 %collective-permute-start = (bf16[4,32,2048]{2,1,0:T(8,128)(2,1)S(1)}, bf16[4,32,2048]{2,1,0:T(8,128)(2,1)S(1)}, u32[]{:S(2)}, u32[]{:S(2)}) collective-permute-start(bf16[4,32,2048]{2,1,0:T(8,128)(2,1)S(1)} %get-tuple-element.40.p1), channel_id=1, source_target_pairs={{0,1},{1,2},{2,3},{3,0},{4,5},{5,6},{6,7},{7,4},{8,9},{9,10},{10,1... | collective-permute-start | bytes 1572872 | tf_op jit(solution)/shard_map/ppermute | solution.py:31
  48.9 3.4 %collective-permute-start.1 = (bf16[4,32,2048]{2,1,0:T(8,128)(2,1)S(1)}, bf16[4,32,2048]{2,1,0:T(8,128)(2,1)S(1)}, u32[]{:S(2)}, u32[]{:S(2)}) collective-permute-start(bf16[4,32,2048]{2,1,0:T(8,128)(2,1)S(1)} %get-tuple-element.41.p2), channel_id=1, source_target_pairs={{0,2},{1,3},{2,0},{3,1},{4,6},{5,7},{6,4},{7,5},{8,10},{9,11},{10,... | collective-permute-start | bytes 1572872 | tf_op jit(solution)/shard_map/ppermute | solution.py:31
  53.1 4.4 %collective-permute-start.2 = (bf16[4,32,2048]{2,1,0:T(8,128)(2,1)S(1)}, bf16[4,32,2048]{2,1,0:T(8,128)(2,1)S(1)}, u32[]{:S(2)}, u32[]{:S(2)}) collective-permute-start(bf16[4,32,2048]{2,1,0:T(8,128)(2,1)S(1)} %get-tuple-element.42.p3), channel_id=1, source_target_pairs={{0,3},{1,0},{2,1},{3,2},{4,7},{5,4},{6,5},{7,6},{8,11},{9,8},{10,9... | collective-permute-start | bytes 1572872 | tf_op jit(solution)/shard_map/ppermute | solution.py:31
  58.4 3.6 %collective-permute-done.e1 = bf16[4,32,2048]{2,1,0:T(8,128)(2,1)S(1)} collective-permute-done((bf16[4,32,2048]{2,1,0:T(8,128)(2,1)S(1)}, bf16[4,32,2048]{2,1,0:T(8,128)(2,1)S(1)}, u32[]{:S(2)}, u32[]{:S(2)}) %collective-permute-start) | collective-permute-done | bytes 524320 | tf_op jit(solution)/shard_map/ppermute | solution.py:31
  62.0 19.6 %collective-permute-done.1.e2 = bf16[4,32,2048]{2,1,0:T(8,128)(2,1)S(1)} collective-permute-done((bf16[4,32,2048]{2,1,0:T(8,128)(2,1)S(1)}, bf16[4,32,2048]{2,1,0:T(8,128)(2,1)S(1)}, u32[]{:S(2)}, u32[]{:S(2)}) %collective-permute-start.1) | collective-permute-done | bytes 524320 | tf_op jit(solution)/shard_map/ppermute | solution.py:31
  84.1 13.6 %collective-permute-start.3 = (bf16[128,2048]{1,0:T(8,128)(2,1)S(1)}, bf16[128,2048]{1,0:T(8,128)(2,1)S(1)}, u32[]{:S(2)}, u32[]{:S(2)}) collective-permute-start(bf16[128,2048]{1,0:T(8,128)(2,1)S(1)} %forward.1.a0), channel_id=1, source_target_pairs={{0,1},{1,2},{2,3},{3,0},{4,5},{5,6},{6,7},{7,4},{8,9},{9,10},{10,1... | collective-permute-start | bytes 1572872 | tf_op jit(solution)/shard_map/ppermute | solution.py:31
  97.7 11.4 %collective-permute-done.3.a1 = bf16[128,2048]{1,0:T(8,128)(2,1)S(1)} collective-permute-done((bf16[128,2048]{1,0:T(8,128)(2,1)S(1)}, bf16[128,2048]{1,0:T(8,128)(2,1)S(1)}, u32[]{:S(2)}, u32[]{:S(2)}) %collective-permute-start.3) | collective-permute-done | bytes 524320 | tf_op jit(solution)/shard_map/ppermute | solution.py:31
  111.1 4.1 %collective-permute-start.6 = (bf16[128,2048]{1,0:T(8,128)(2,1)S(1)}, bf16[128,2048]{1,0:T(8,128)(2,1)S(1)}, u32[]{:S(2)}, u32[]{:S(2)}) collective-permute-start(bf16[128,2048]{1,0:T(8,128)(2,1)S(1)} %forward.1.a0), channel_id=1, source_target_pairs={{0,2},{1,3},{2,0},{3,1},{4,6},{5,7},{6,4},{7,5},{8,10},{9,11},{10,... | collective-permute-start | bytes 1572872 | tf_op jit(solution)/shard_map/ppermute | solution.py:31
  115.2 4.5 %collective-permute-start.7 = (bf16[128,2048]{1,0:T(8,128)(2,1)S(1)}, bf16[128,2048]{1,0:T(8,128)(2,1)S(1)}, u32[]{:S(2)}, u32[]{:S(2)}) collective-permute-start(bf16[128,2048]{1,0:T(8,128)(2,1)S(1)} %forward.1.a0), channel_id=1, source_target_pairs={{0,3},{1,0},{2,1},{3,2},{4,7},{5,4},{6,5},{7,6},{8,11},{9,8},{10,9... | collective-permute-start | bytes 1572872 | tf_op jit(solution)/shard_map/ppermute | solution.py:31
  124.1 7.8 %backward.1 = (bf16[3,32,2048]{2,1,0:T(8,128)(2,1)S(1)}, bf16[3,32,2048]{2,1,0:T(8,128)(2,1)S(1)}, bf16[3,32,2048]{2,1,0:T(8,128)(2,1)S(1)}, bf16[3,32,2048]{2,1,0:T(8,128)(2,1)S(1)}) custom-call(s32[5]{0:T(128)S(1)} %stack.23.pos_ref, bf16[4,32,2048]{2,1,0:T(8,128)(2,1)S(1)} %get-tuple-element.39.e0.p0, bf16[4,32,2048]{2,1,0:T(8,128)(2,1)S(1)} %collective-permute-done.e1, ...), custom_call_target="tpu_custom_call" | custom-call | tf_op jit(solution)/shard_map/backward/pallas_call | solution.py:180
  131.9 3.0 %collective-permute-start.5 = (bf16[3,32,2048]{2,1,0:T(8,128)(2,1)S(1)}, bf16[3,32,2048]{2,1,0:T(8,128)(2,1)S(1)}, u32[]{:S(2)}, u32[]{:S(2)}) collective-permute-start(bf16[3,32,2048]{2,1,0:T(8,128)(2,1)S(1)} %get-tuple-element.45), channel_id=1, source_target_pairs={{0,1},{1,2},{2,3},{3,0},{4,5},{5,6},{6,7},{7,4},{8,9},{9,10},{10,1... | collective-permute-start | bytes 1179656 | tf_op jit(solution)/shard_map/ppermute | solution.py:31
  135.0 4.9 %collective-permute-done.6.a2 = bf16[128,2048]{1,0:T(8,128)(2,1)S(1)} collective-permute-done((bf16[128,2048]{1,0:T(8,128)(2,1)S(1)}, bf16[128,2048]{1,0:T(8,128)(2,1)S(1)}, u32[]{:S(2)}, u32[]{:S(2)}) %collective-permute-start.6) | collective-permute-done | bytes 524320 | tf_op jit(solution)/shard_map/ppermute | solution.py:31
  140.4 9.6 %collective-permute-done.5.h1 = bf16[3,32,2048]{2,1,0:T(8,128)(2,1)S(1)} collective-permute-done((bf16[3,32,2048]{2,1,0:T(8,128)(2,1)S(1)}, bf16[3,32,2048]{2,1,0:T(8,128)(2,1)S(1)}, u32[]{:S(2)}, u32[]{:S(2)}) %collective-permute-start.5) | collective-permute-done | bytes 393248 | tf_op jit(solution)/shard_map/ppermute | solution.py:31
  154.4 4.1 %collective-permute-done.8 = f32[4,4,4,16,512]{4,3,2,1,0:T(8,128)S(1)} collective-permute-done((f32[4,4,4,16,512]{4,3,2,1,0:T(8,128)S(1)}, f32[4,4,4,16,512]{4,3,2,1,0:T(8,128)S(1)}, u32[]{:S(2)}, u32[]{:S(2)}) %collective-permute-start.8) | collective-permute-done | bytes 2097184 | tf_op jit(solution)/shard_map/ppermute | solution.py:242
  160.5 7.5 %all-to-all-start.1 = ((f32[16,4,16,512]{3,2,1,0:T(8,128)}), f32[16,4,16,512]{3,2,1,0:T(8,128)}, u32[]{:S(2)}, u32[]{:S(2)}) async-start(f32[16,4,16,512]{3,2,1,0:T(8,128)} %bitcast.23), calls=%async_computation.1 | async-start | bytes 4194304 | tf_op jit(solution)/shard_map/all_to_all | solution.py:243
  168.0 13.3 %collective-permute-start.10 = (bf16[3,32,2048]{2,1,0:T(8,128)(2,1)}, bf16[3,32,2048]{2,1,0:T(8,128)(2,1)S(1)}, u32[]{:S(2)}, u32[]{:S(2)}) collective-permute-start(bf16[3,32,2048]{2,1,0:T(8,128)(2,1)} %copy-done.19), channel_id=1, source_target_pairs={{0,3},{1,0},{2,1},{3,2},{4,7},{5,4},{6,5},{7,6},{8,11},{9,8},{10,9... | collective-permute-start | bytes 1179656 | tf_op jit(solution)/shard_map/ppermute | solution.py:31
  187.6 3.1 %project.1 = bf16[16,32,512]{2,1,0:T(8,128)(2,1)} custom-call(s32[5]{0:T(128)S(1)} %stack.23.pos_ref, bf16[128,2048]{1,0:T(8,128)(2,1)S(1)} %forward.1.a0, bf16[128,2048]{1,0:T(8,128)(2,1)S(1)} %collective-permute-done.3.a1, bf16[128,2048]{1,0:T(8,128)(2,1)S(1)} %collective-permute-done.6.a2, bf16[128,2048]{1,0:T(8,128)(2,1)S(1)} %collective-permute-done.7.a3, ...), custom_call_target="tpu_custom_call" | custom-call | tf_op jit(solution)/shard_map/project/pallas_call | solution.py:180
  191.2 15.7 %collective-permute-done.9.h2 = bf16[3,32,2048]{2,1,0:T(8,128)(2,1)} collective-permute-done((bf16[3,32,2048]{2,1,0:T(8,128)(2,1)}, bf16[3,32,2048]{2,1,0:T(8,128)(2,1)}, u32[]{:S(2)}, u32[]{:S(2)}) %collective-permute-start.9) | collective-permute-done | bytes 393248 | tf_op jit(solution)/shard_map/ppermute | solution.py:31
  206.9 3.4 %unpack.1 = (bf16[4,32,2048]{2,1,0:T(8,128)(2,1)}, bf16[4,32,2048]{2,1,0:T(8,128)(2,1)}, bf16[4,32,2048]{2,1,0:T(8,128)(2,1)}) custom-call(s32[5]{0:T(128)S(1)} %stack.23.pos_ref, bf16[3,32,2048]{2,1,0:T(8,128)(2,1)S(1)} %get-tuple-element.53.h0, bf16[3,32,2048]{2,1,0:T(8,128)(2,1)S(1)} %collective-permute-done.5.h1, ...), custom_call_target="tpu_custom_call" | custom-call | tf_op jit(solution)/shard_map/unpack/pallas_call | solution.py:180
  212.1 4.8 %collective-permute-start.11 = (f32[16,512]{1,0:T(8,128)S(1)}, f32[16,512]{1,0:T(8,128)S(1)}, u32[]{:S(2)}, u32[]{:S(2)}) collective-permute-start(f32[16,512]{1,0:T(8,128)S(1)} %get-tuple-element.65), channel_id=1, source_target_pairs={{0,32},{32,64},{64,96},{96,0},{1,33},{33,65},{65,97},{97,1},{2,34}... | collective-permute-start | bytes 98312 | tf_op jit(solution)/shard_map/ppermute | solution.py:31
  216.9 9.1 %collective-permute-start.12 = (f32[16,512]{1,0:T(8,128)S(1)}, f32[16,512]{1,0:T(8,128)S(1)}, u32[]{:S(2)}, u32[]{:S(2)}) collective-permute-start(f32[16,512]{1,0:T(8,128)S(1)} %get-tuple-element.67), channel_id=1, source_target_pairs={{0,64},{32,96},{64,0},{96,32},{1,65},{33,97},{65,1},{97,33},{2,66}... | collective-permute-start | bytes 98312 | tf_op jit(solution)/shard_map/ppermute | solution.py:31
  231.8 3.9 %collective-permute-done.13 = f32[16,512]{1,0:T(8,128)S(1)} collective-permute-done((f32[16,512]{1,0:T(8,128)S(1)}, f32[16,512]{1,0:T(8,128)S(1)}, u32[]{:S(2)}, u32[]{:S(2)}) %collective-permute-start.13) | collective-permute-done | bytes 32800 | tf_op jit(solution)/shard_map/ppermute | solution.py:31
  (65 shorter events, 40.8 us)
Async XLA Ops:
  8.6 32.7 %all-to-all-start = ((bf16[16,16,512]{2,1,0:T(8,128)(2,1)}), bf16[16,16,512]{2,1,0:T(8,128)(2,1)S(1)}, u32[]{:S(2)}, u32[]{:S(2)}) async-start(bf16[16,16,512]{2,1,0:T(8,128)(2,1)} %broadcast_in_dim.2), calls=%async_computation | async-start | bytes 524288 | tf_op jit(solution)/shard_map/all_to_all | solution.py:197
  23.8 85.4 %all-gather.2.cloned.1.call-start = ((), (), s32[]{:S(2)}) async-start(), calls=%async_computation.2 | async-start | bytes 4456448 | tf_op jit(solution)/shard_map/all_gather | solution.py:206
  42.1 19.9 %collective-permute-start = (bf16[4,32,2048]{2,1,0:T(8,128)(2,1)S(1)}, bf16[4,32,2048]{2,1,0:T(8,128)(2,1)S(1)}, u32[]{:S(2)}, u32[]{:S(2)}) collective-permute-start(bf16[4,32,2048]{2,1,0:T(8,128)(2,1)S(1)} %get-tuple-element.40.p1), channel_id=1, source_target_pairs={{0,1},{1,2},{2,3},{3,0},{4,5},{5,6},{6,7},{7,4},{8,9},{9,10},{10,1... | collective-permute-start | bytes 1572872 | tf_op jit(solution)/shard_map/ppermute | solution.py:31
  48.9 32.7 %collective-permute-start.1 = (bf16[4,32,2048]{2,1,0:T(8,128)(2,1)S(1)}, bf16[4,32,2048]{2,1,0:T(8,128)(2,1)S(1)}, u32[]{:S(2)}, u32[]{:S(2)}) collective-permute-start(bf16[4,32,2048]{2,1,0:T(8,128)(2,1)S(1)} %get-tuple-element.41.p2), channel_id=1, source_target_pairs={{0,2},{1,3},{2,0},{3,1},{4,6},{5,7},{6,4},{7,5},{8,10},{9,11},{10,... | collective-permute-start | bytes 1572872 | tf_op jit(solution)/shard_map/ppermute | solution.py:31
  53.1 28.5 %collective-permute-start.2 = (bf16[4,32,2048]{2,1,0:T(8,128)(2,1)S(1)}, bf16[4,32,2048]{2,1,0:T(8,128)(2,1)S(1)}, u32[]{:S(2)}, u32[]{:S(2)}) collective-permute-start(bf16[4,32,2048]{2,1,0:T(8,128)(2,1)S(1)} %get-tuple-element.42.p3), channel_id=1, source_target_pairs={{0,3},{1,0},{2,1},{3,2},{4,7},{5,4},{6,5},{7,6},{8,11},{9,8},{10,9... | collective-permute-start | bytes 1572872 | tf_op jit(solution)/shard_map/ppermute | solution.py:31
  81.6 16.1 %copy-start.6 = (bf16[4,32,2048]{2,1,0:T(8,128)(2,1)}, bf16[4,32,2048]{2,1,0:T(8,128)(2,1)S(1)}, u32[]{:S(2)}) copy-start(bf16[4,32,2048]{2,1,0:T(8,128)(2,1)S(1)} %collective-permute-done.2.e3) | copy-start | bytes 1572868
  84.1 25.1 %collective-permute-start.3 = (bf16[128,2048]{1,0:T(8,128)(2,1)S(1)}, bf16[128,2048]{1,0:T(8,128)(2,1)S(1)}, u32[]{:S(2)}, u32[]{:S(2)}) collective-permute-start(bf16[128,2048]{1,0:T(8,128)(2,1)S(1)} %forward.1.a0), channel_id=1, source_target_pairs={{0,1},{1,2},{2,3},{3,0},{4,5},{5,6},{6,7},{7,4},{8,9},{9,10},{10,1... | collective-permute-start | bytes 1572872 | tf_op jit(solution)/shard_map/ppermute | solution.py:31
  109.2 10.6 %collective-permute-start.4 = (bf16[4,4,4,4,16,512]{5,4,3,2,1,0:T(8,128)(2,1)}, bf16[4,4,4,4,16,512]{5,4,3,2,1,0:T(8,128)(2,1)S(1)}, u32[]{:S(2)}, u32[]{:S(2)}) collective-permute-start(bf16[4,4,4,4,16,512]{5,4,3,2,1,0:T(8,128)(2,1)} %bitcast.20), channel_id=1, source_target_pairs={{0,4},{4,0},{1,5},{5,1},{2,6},{6,2},{3,7},{7,3},{8,12},{12,8},{9,1... | collective-permute-start | bytes 12582920 | tf_op jit(solution)/shard_map/ppermute | solution.py:214
  111.1 28.8 %collective-permute-start.6 = (bf16[128,2048]{1,0:T(8,128)(2,1)S(1)}, bf16[128,2048]{1,0:T(8,128)(2,1)S(1)}, u32[]{:S(2)}, u32[]{:S(2)}) collective-permute-start(bf16[128,2048]{1,0:T(8,128)(2,1)S(1)} %forward.1.a0), channel_id=1, source_target_pairs={{0,2},{1,3},{2,0},{3,1},{4,6},{5,7},{6,4},{7,5},{8,10},{9,11},{10,... | collective-permute-start | bytes 1572872 | tf_op jit(solution)/shard_map/ppermute | solution.py:31
  115.2 25.2 %collective-permute-start.7 = (bf16[128,2048]{1,0:T(8,128)(2,1)S(1)}, bf16[128,2048]{1,0:T(8,128)(2,1)S(1)}, u32[]{:S(2)}, u32[]{:S(2)}) collective-permute-start(bf16[128,2048]{1,0:T(8,128)(2,1)S(1)} %forward.1.a0), channel_id=1, source_target_pairs={{0,3},{1,0},{2,1},{3,2},{4,7},{5,4},{6,5},{7,6},{8,11},{9,8},{10,9... | collective-permute-start | bytes 1572872 | tf_op jit(solution)/shard_map/ppermute | solution.py:31
  124.0 7.9 %copy-start.2 = (bf16[4,4,4,4,16,512]{5,4,3,2,1,0:T(8,128)(2,1)}, bf16[4,4,4,4,16,512]{5,4,3,2,1,0:T(8,128)(2,1)S(1)}, u32[]{:S(2)}) copy-start(bf16[4,4,4,4,16,512]{5,4,3,2,1,0:T(8,128)(2,1)S(1)} %collective-permute-done.4.other_ref) | copy-start | bytes 12582916
  124.0 25.9 %copy-start.13 = (bf16[4,32,2048]{2,1,0:T(8,128)(2,1)S(1)}, bf16[4,32,2048]{2,1,0:T(8,128)(2,1)}, u32[]{:S(2)}) copy-start(bf16[4,32,2048]{2,1,0:T(8,128)(2,1)} %copy-done.12) | copy-start | bytes 1572868
  124.0 25.9 %copy-start.15 = (bf16[4,32,2048]{2,1,0:T(8,128)(2,1)S(1)}, bf16[4,32,2048]{2,1,0:T(8,128)(2,1)}, u32[]{:S(2)}) copy-start(bf16[4,32,2048]{2,1,0:T(8,128)(2,1)} %copy-done.14) | copy-start | bytes 1572868
  124.0 25.9 %copy-start.17 = (bf16[4,32,2048]{2,1,0:T(8,128)(2,1)S(1)}, bf16[4,32,2048]{2,1,0:T(8,128)(2,1)}, u32[]{:S(2)}) copy-start(bf16[4,32,2048]{2,1,0:T(8,128)(2,1)} %copy-done.16) | copy-start | bytes 1572868
  131.9 28.6 %copy-start.18 = (bf16[3,32,2048]{2,1,0:T(8,128)(2,1)}, bf16[3,32,2048]{2,1,0:T(8,128)(2,1)S(1)}, u32[]{:S(2)}) copy-start(bf16[3,32,2048]{2,1,0:T(8,128)(2,1)S(1)} %get-tuple-element.55) | copy-start | bytes 1179652
  131.9 28.6 %copy-start.19 = (bf16[3,32,2048]{2,1,0:T(8,128)(2,1)}, bf16[3,32,2048]{2,1,0:T(8,128)(2,1)S(1)}, u32[]{:S(2)}) copy-start(bf16[3,32,2048]{2,1,0:T(8,128)(2,1)S(1)} %get-tuple-element.56) | copy-start | bytes 1179652
  131.9 18.0 %collective-permute-start.5 = (bf16[3,32,2048]{2,1,0:T(8,128)(2,1)S(1)}, bf16[3,32,2048]{2,1,0:T(8,128)(2,1)S(1)}, u32[]{:S(2)}, u32[]{:S(2)}) collective-permute-start(bf16[3,32,2048]{2,1,0:T(8,128)(2,1)S(1)} %get-tuple-element.45), channel_id=1, source_target_pairs={{0,1},{1,2},{2,3},{3,0},{4,5},{5,6},{6,7},{7,4},{8,9},{9,10},{10,1... | collective-permute-start | bytes 1179656 | tf_op jit(solution)/shard_map/ppermute | solution.py:31
  152.4 6.1 %collective-permute-start.8 = (f32[4,4,4,16,512]{4,3,2,1,0:T(8,128)S(1)}, f32[4,4,4,16,512]{4,3,2,1,0:T(8,128)S(1)}, u32[]{:S(2)}, u32[]{:S(2)}) collective-permute-start(f32[4,4,4,16,512]{4,3,2,1,0:T(8,128)S(1)} %get-tuple-element.52), channel_id=1, source_target_pairs={{0,4},{4,0},{1,5},{5,1},{2,6},{6,2},{3,7},{7,3},{8,12},{12,8},{9,1... | collective-permute-start | bytes 6291464 | tf_op jit(solution)/shard_map/ppermute | solution.py:242
  160.5 49.7 %all-to-all-start.1 = ((f32[16,4,16,512]{3,2,1,0:T(8,128)}), f32[16,4,16,512]{3,2,1,0:T(8,128)}, u32[]{:S(2)}, u32[]{:S(2)}) async-start(f32[16,4,16,512]{3,2,1,0:T(8,128)} %bitcast.23), calls=%async_computation.1 | async-start | bytes 4194304 | tf_op jit(solution)/shard_map/all_to_all | solution.py:243
  168.0 23.2 %collective-permute-start.10 = (bf16[3,32,2048]{2,1,0:T(8,128)(2,1)}, bf16[3,32,2048]{2,1,0:T(8,128)(2,1)S(1)}, u32[]{:S(2)}, u32[]{:S(2)}) collective-permute-start(bf16[3,32,2048]{2,1,0:T(8,128)(2,1)} %copy-done.19), channel_id=1, source_target_pairs={{0,3},{1,0},{2,1},{3,2},{4,7},{5,4},{6,5},{7,6},{8,11},{9,8},{10,9... | collective-permute-start | bytes 1179656 | tf_op jit(solution)/shard_map/ppermute | solution.py:31
  181.3 25.6 %collective-permute-start.9 = (bf16[3,32,2048]{2,1,0:T(8,128)(2,1)}, bf16[3,32,2048]{2,1,0:T(8,128)(2,1)}, u32[]{:S(2)}, u32[]{:S(2)}) collective-permute-start(bf16[3,32,2048]{2,1,0:T(8,128)(2,1)} %copy-done.18), channel_id=1, source_target_pairs={{0,2},{1,3},{2,0},{3,1},{4,6},{5,7},{6,4},{7,5},{8,10},{9,11},{10,... | collective-permute-start | bytes 1179656 | tf_op jit(solution)/shard_map/ppermute | solution.py:31
  212.1 16.9 %collective-permute-start.11 = (f32[16,512]{1,0:T(8,128)S(1)}, f32[16,512]{1,0:T(8,128)S(1)}, u32[]{:S(2)}, u32[]{:S(2)}) collective-permute-start(f32[16,512]{1,0:T(8,128)S(1)} %get-tuple-element.65), channel_id=1, source_target_pairs={{0,32},{32,64},{64,96},{96,0},{1,33},{33,65},{65,97},{97,1},{2,34}... | collective-permute-start | bytes 98312 | tf_op jit(solution)/shard_map/ppermute | solution.py:31
  216.9 14.9 %collective-permute-start.12 = (f32[16,512]{1,0:T(8,128)S(1)}, f32[16,512]{1,0:T(8,128)S(1)}, u32[]{:S(2)}, u32[]{:S(2)}) collective-permute-start(f32[16,512]{1,0:T(8,128)S(1)} %get-tuple-element.67), channel_id=1, source_target_pairs={{0,64},{32,96},{64,0},{96,32},{1,65},{33,97},{65,1},{97,33},{2,66}... | collective-permute-start | bytes 98312 | tf_op jit(solution)/shard_map/ppermute | solution.py:31
  226.0 9.7 %collective-permute-start.13 = (f32[16,512]{1,0:T(8,128)S(1)}, f32[16,512]{1,0:T(8,128)S(1)}, u32[]{:S(2)}, u32[]{:S(2)}) collective-permute-start(f32[16,512]{1,0:T(8,128)S(1)} %get-tuple-element.66), channel_id=1, source_target_pairs={{0,96},{32,0},{64,32},{96,64},{1,97},{33,1},{65,33},{97,65},{2,98}... | collective-permute-start | bytes 98312 | tf_op jit(solution)/shard_map/ppermute | solution.py:31
  (14 other events, 18.4 us)
Sparse Core Ops, SparseCore 0:
  42.2 62.7 all-gather.1

commit v2 on v1

--- a/solution.py
+++ b/solution.py
@@ -225,9 +225,9 @@
         ],
         40,
     )
+    *back, attended_all[0] = lax.optimization_barrier((*back, attended_all[0]))
     home = [back[0]] + [shift(back[n], "s", n) for n in (1, 2, 3)]
 
-    home[1], *attended_all = lax.optimization_barrier((home[1], *attended_all))
     quarter = jax.ShapeDtypeStruct((4, 4, 4, 16, 512), F32)
     keep, send = call(
         weight_kernel, "weight", [quarter] * 2, (pos, *attended_all, *sent), VMEM,
@@ -256,9 +256,7 @@
         unpack_kernel, "unpack", [jax.ShapeDtypeStruct((4, 32, 2048), BF)] * 3, (pos, *home), VMEM,
         [pltpu.VMEM((4, 3, 32, 2048), BF), pltpu.VMEM((4, 4, 32, 512), F32), dma((4,))], 32,
     )
-    parts, block_out, query_grad, key_grad, value_grad = lax.optimization_barrier(
-        (parts, block_out, query_grad, key_grad, value_grad)
-    )
+    parts, block_out = lax.optimization_barrier((parts, block_out))
     plane_sum = parts.sum(axis=0)
     weight_grad = None
     for step in range(4):

time: 244 us -> 232 us (0.951)
  the two profiles are of different devices: /device:TPU:2 before, /device:TPU:32 now
where the time goes in v2:
time: 232 us; the launch traced here: 231 us
  waiting for transfers between devices  102 us (44%)
  starting transfers between devices  71.5 us (31%)
  Pallas kernels  21.2 us (9%)
  local copies, waits for them, and re-layouts  17.5 us (8%)
  between operations  14.4 us (6%)
  other arithmetic  4.44 us (2%)
    ppermute x12, waiting for transfers between devices, shift(): return lax.ppermute(array, axis, [(i, (i + step) % 4) for i in range(4)])  70.2 us
    ppermute x12, starting transfers between devices, shift(): return lax.ppermute(array, axis, [(i, (i + step) % 4) for i in range(4)])  45.3 us
    pallas_call x6, Pallas kernels, call(): pl.pallas_call(kernel, out_shape=out_shape, in_specs=[SMEM] + [ANY] * (le...  21.2 us
    unnamed x42, local copies, waits for them, and re-layouts  16 us
    all_to_all x1, starting transfers between devices, per_device(): column = lax.all_to_all(spread, ('s', 'zh'), 0, 0)  15.2 us
    all_to_all x1, waiting for transfers between devices, per_device(): column = lax.all_to_all(spread, ('s', 'zh'), 0, 0)  14.1 us
    all_to_all x1, waiting for transfers between devices, per_device(): parts = lax.all_to_all(chip_sum.reshape(16, 4, 16, 512), ('x', 'y'), 0, 0)  12 us
    all_to_all x1, starting transfers between devices, per_device(): parts = lax.all_to_all(chip_sum.reshape(16, 4, 16, 512), ('x', 'y'), 0, 0)  7.09 us
  transfers between devices with their start and end apart: 17, of which 12 were waited for; matrix products, arithmetic and copies ran while one was open for 1% of the time, Pallas kernels for 8%

profile of v2, /device:TPU:32, one launch (start us, length us, event | category | flops | bytes accessed | tf_op | source)
XLA Modules:
  0.0 231.2 jit_solution(11388320406191105293)
XLA Ops:
  8.6 15.2 %all-to-all-start = ((bf16[16,16,512]{2,1,0:T(8,128)(2,1)}), bf16[16,16,512]{2,1,0:T(8,128)(2,1)S(1)}, u32[]{:S(2)}, u32[]{:S(2)}) async-start(bf16[16,16,512]{2,1,0:T(8,128)(2,1)} %broadcast_in_dim.2), calls=%async_computation | async-start | bytes 524288 | tf_op jit(solution)/shard_map/all_to_all | solution.py:197
  29.5 14.1 %all-to-all-done = bf16[16,16,512]{2,1,0:T(8,128)(2,1)S(1)} async-done(((bf16[16,16,512]{2,1,0:T(8,128)(2,1)}), bf16[16,16,512]{2,1,0:T(8,128)(2,1)S(1)}, u32[]{:S(2)}, u32[]{:S(2)}) %all-to-all-start) | async-done | bytes 262176 | tf_op jit(solution)/shard_map/all_to_all | solution.py:197
  44.3 3.6 %collective-permute-start = (bf16[4,32,2048]{2,1,0:T(8,128)(2,1)S(1)}, bf16[4,32,2048]{2,1,0:T(8,128)(2,1)S(1)}, u32[]{:S(2)}, u32[]{:S(2)}) collective-permute-start(bf16[4,32,2048]{2,1,0:T(8,128)(2,1)S(1)} %get-tuple-element.37.p1), channel_id=1, source_target_pairs={{0,1},{1,2},{2,3},{3,0},{4,5},{5,6},{6,7},{7,4},{8,9},{9,10},{10,1... | collective-permute-start | bytes 1572872 | tf_op jit(solution)/shard_map/ppermute | solution.py:31
  51.4 3.7 %collective-permute-start.2 = (bf16[4,32,2048]{2,1,0:T(8,128)(2,1)S(1)}, bf16[4,32,2048]{2,1,0:T(8,128)(2,1)S(1)}, u32[]{:S(2)}, u32[]{:S(2)}) collective-permute-start(bf16[4,32,2048]{2,1,0:T(8,128)(2,1)S(1)} %get-tuple-element.39.p3), channel_id=1, source_target_pairs={{0,3},{1,0},{2,1},{3,2},{4,7},{5,4},{6,5},{7,6},{8,11},{9,8},{10,9... | collective-permute-start | bytes 1572872 | tf_op jit(solution)/shard_map/ppermute | solution.py:31
  56.0 26.7 %collective-permute-done.e1 = bf16[4,32,2048]{2,1,0:T(8,128)(2,1)S(1)} collective-permute-done((bf16[4,32,2048]{2,1,0:T(8,128)(2,1)S(1)}, bf16[4,32,2048]{2,1,0:T(8,128)(2,1)S(1)}, u32[]{:S(2)}, u32[]{:S(2)}) %collective-permute-start) | collective-permute-done | bytes 524320 | tf_op jit(solution)/shard_map/ppermute | solution.py:31
  82.7 7.6 %collective-permute-done.1.e2 = bf16[4,32,2048]{2,1,0:T(8,128)(2,1)S(1)} collective-permute-done((bf16[4,32,2048]{2,1,0:T(8,128)(2,1)S(1)}, bf16[4,32,2048]{2,1,0:T(8,128)(2,1)S(1)}, u32[]{:S(2)}, u32[]{:S(2)}) %collective-permute-start.1) | collective-permute-done | bytes 524320 | tf_op jit(solution)/shard_map/ppermute | solution.py:31
  91.4 2.4 %forward.1.a0 = bf16[128,2048]{1,0:T(8,128)(2,1)S(1)} custom-call(s32[5]{0:T(128)S(1)} %stack.23.pos_ref, bf16[4,32,2048]{2,1,0:T(8,128)(2,1)S(1)} %get-tuple-element.36.e0.p0, bf16[4,32,2048]{2,1,0:T(8,128)(2,1)S(1)} %collective-permute-done.e1, bf16[4,32,2048]{2,1,0:T(8,128)(2,1)S(1)} %collective-permute-done.1.e2, ...), custom_call_target="tpu_custom_call" | custom-call | tf_op jit(solution)/shard_map/forward/pallas_call | solution.py:180
  95.8 13.9 %collective-permute-done.3.a1 = bf16[128,2048]{1,0:T(8,128)(2,1)S(1)} collective-permute-done((bf16[128,2048]{1,0:T(8,128)(2,1)S(1)}, bf16[128,2048]{1,0:T(8,128)(2,1)S(1)}, u32[]{:S(2)}, u32[]{:S(2)}) %collective-permute-start.3) | collective-permute-done | bytes 524320 | tf_op jit(solution)/shard_map/ppermute | solution.py:31
  113.6 3.7 %collective-permute-start.6 = (bf16[128,2048]{1,0:T(8,128)(2,1)S(1)}, bf16[128,2048]{1,0:T(8,128)(2,1)S(1)}, u32[]{:S(2)}, u32[]{:S(2)}) collective-permute-start(bf16[128,2048]{1,0:T(8,128)(2,1)S(1)} %forward.1.a0), channel_id=1, source_target_pairs={{0,3},{1,0},{2,1},{3,2},{4,7},{5,4},{6,5},{7,6},{8,11},{9,8},{10,9... | collective-permute-start | bytes 1572872 | tf_op jit(solution)/shard_map/ppermute | solution.py:31
  119.0 2.2 copy-done
  123.3 8.5 %backward.1 = (bf16[3,32,2048]{2,1,0:T(8,128)(2,1)S(1)}, bf16[3,32,2048]{2,1,0:T(8,128)(2,1)S(1)}, bf16[3,32,2048]{2,1,0:T(8,128)(2,1)S(1)}, bf16[3,32,2048]{2,1,0:T(8,128)(2,1)}) custom-call(s32[5]{0:T(128)S(1)} %stack.23.pos_ref, bf16[4,32,2048]{2,1,0:T(8,128)(2,1)S(1)} %get-tuple-element.36.e0.p0, bf16[4,32,2048]{2,1,0:T(8,128)(2,1)S(1)} %collective-permute-done.e1, ...), custom_call_target="tpu_custom_call" | custom-call | tf_op jit(solution)/shard_map/backward/pallas_call | solution.py:180
  131.8 16.3 %collective-permute-done.5.a2 = bf16[128,2048]{1,0:T(8,128)(2,1)S(1)} collective-permute-done((bf16[128,2048]{1,0:T(8,128)(2,1)S(1)}, bf16[128,2048]{1,0:T(8,128)(2,1)S(1)}, u32[]{:S(2)}, u32[]{:S(2)}) %collective-permute-start.5) | collective-permute-done | bytes 524320 | tf_op jit(solution)/shard_map/ppermute | solution.py:31
  149.4 2.5 %weight.1 = (f32[4,4,4,16,512]{4,3,2,1,0:T(8,128)S(1)}, f32[4,4,4,16,512]{4,3,2,1,0:T(8,128)S(1)}) custom-call(s32[5]{0:T(128)S(1)} %stack.23.pos_ref, bf16[128,2048]{1,0:T(8,128)(2,1)S(1)} %forward.1.a0, bf16[128,2048]{1,0:T(8,128)(2,1)S(1)} %collective-permute-done.3.a1, bf16[128,2048]{1,0:T(8,128)(2,1)S(1)} %collective-permute-done.5.a2, ...), custom_call_target="tpu_custom_call" | custom-call | tf_op jit(solution)/shard_map/weight/pallas_call | solution.py:180
  153.8 4.1 %collective-permute-done.7 = f32[4,4,4,16,512]{4,3,2,1,0:T(8,128)S(1)} collective-permute-done((f32[4,4,4,16,512]{4,3,2,1,0:T(8,128)S(1)}, f32[4,4,4,16,512]{4,3,2,1,0:T(8,128)S(1)}, u32[]{:S(2)}, u32[]{:S(2)}) %collective-permute-start.7) | collective-permute-done | bytes 2097184 | tf_op jit(solution)/shard_map/ppermute | solution.py:242
  160.0 7.1 %all-to-all-start.1 = ((f32[16,4,16,512]{3,2,1,0:T(8,128)}), f32[16,4,16,512]{3,2,1,0:T(8,128)}, u32[]{:S(2)}, u32[]{:S(2)}) async-start(f32[16,4,16,512]{3,2,1,0:T(8,128)} %bitcast.23), calls=%async_computation.1 | async-start | bytes 4194304 | tf_op jit(solution)/shard_map/all_to_all | solution.py:243
  169.0 3.9 %collective-permute-start.8 = (bf16[3,32,2048]{2,1,0:T(8,128)(2,1)}, bf16[3,32,2048]{2,1,0:T(8,128)(2,1)S(1)}, u32[]{:S(2)}, u32[]{:S(2)}) collective-permute-start(bf16[3,32,2048]{2,1,0:T(8,128)(2,1)} %copy-done.19), channel_id=1, source_target_pairs={{0,1},{1,2},{2,3},{3,0},{4,5},{5,6},{6,7},{7,4},{8,9},{9,10},{10,1... | collective-permute-start | bytes 1179656 | tf_op jit(solution)/shard_map/ppermute | solution.py:31
  172.9 5.9 %collective-permute-start.9 = (bf16[3,32,2048]{2,1,0:T(8,128)(2,1)}, bf16[3,32,2048]{2,1,0:T(8,128)(2,1)}, u32[]{:S(2)}, u32[]{:S(2)}) collective-permute-start(bf16[3,32,2048]{2,1,0:T(8,128)(2,1)} %copy-done.18), channel_id=1, source_target_pairs={{0,2},{1,3},{2,0},{3,1},{4,6},{5,7},{6,4},{7,5},{8,10},{9,11},{10,... | collective-permute-start | bytes 1179656 | tf_op jit(solution)/shard_map/ppermute | solution.py:31
  183.2 3.1 %project.1 = bf16[16,32,512]{2,1,0:T(8,128)(2,1)} custom-call(s32[5]{0:T(128)S(1)} %stack.23.pos_ref, bf16[128,2048]{1,0:T(8,128)(2,1)S(1)} %forward.1.a0, bf16[128,2048]{1,0:T(8,128)(2,1)S(1)} %collective-permute-done.3.a1, bf16[128,2048]{1,0:T(8,128)(2,1)S(1)} %collective-permute-done.5.a2, bf16[128,2048]{1,0:T(8,128)(2,1)S(1)} %collective-permute-done.6.a3, ...), custom_call_target="tpu_custom_call" | custom-call | tf_op jit(solution)/shard_map/project/pallas_call | solution.py:180
  186.3 12.0 %all-to-all-done.1 = f32[16,4,16,512]{3,2,1,0:T(8,128)} async-done(((f32[16,4,16,512]{3,2,1,0:T(8,128)}), f32[16,4,16,512]{3,2,1,0:T(8,128)}, u32[]{:S(2)}, u32[]{:S(2)}) %all-to-all-start.1) | async-done | bytes 2097184 | tf_op jit(solution)/shard_map/all_to_all | solution.py:243
  200.1 4.8 %collective-permute-start.11 = (f32[16,512]{1,0:T(8,128)S(1)}, f32[16,512]{1,0:T(8,128)S(1)}, u32[]{:S(2)}, u32[]{:S(2)}) collective-permute-start(f32[16,512]{1,0:T(8,128)S(1)} %get-tuple-element.59), channel_id=1, source_target_pairs={{0,32},{32,64},{64,96},{96,0},{1,33},{33,65},{65,97},{97,1},{2,34}... | collective-permute-start | bytes 98312 | tf_op jit(solution)/shard_map/ppermute | solution.py:31
  204.9 9.1 %collective-permute-start.12 = (f32[16,512]{1,0:T(8,128)S(1)}, f32[16,512]{1,0:T(8,128)S(1)}, u32[]{:S(2)}, u32[]{:S(2)}) collective-permute-start(f32[16,512]{1,0:T(8,128)S(1)} %get-tuple-element.61), channel_id=1, source_target_pairs={{0,64},{32,96},{64,0},{96,32},{1,65},{33,97},{65,1},{97,33},{2,66}... | collective-permute-start | bytes 98312 | tf_op jit(solution)/shard_map/ppermute | solution.py:31
  214.0 3.0 %collective-permute-start.13 = (f32[16,512]{1,0:T(8,128)S(1)}, f32[16,512]{1,0:T(8,128)S(1)}, u32[]{:S(2)}, u32[]{:S(2)}) collective-permute-start(f32[16,512]{1,0:T(8,128)S(1)} %get-tuple-element.60), channel_id=1, source_target_pairs={{0,96},{32,0},{64,32},{96,64},{1,97},{33,1},{65,33},{97,65},{2,98}... | collective-permute-start | bytes 98312 | tf_op jit(solution)/shard_map/ppermute | solution.py:31
  217.0 3.4 %unpack.1 = (bf16[4,32,2048]{2,1,0:T(8,128)(2,1)}, bf16[4,32,2048]{2,1,0:T(8,128)(2,1)}, bf16[4,32,2048]{2,1,0:T(8,128)(2,1)}) custom-call(s32[5]{0:T(128)S(1)} %stack.23.pos_ref, bf16[3,32,2048]{2,1,0:T(8,128)(2,1)S(1)} %get-tuple-element.51.h0, bf16[3,32,2048]{2,1,0:T(8,128)(2,1)S(1)} %collective-permute-done.8.h1, ...), custom_call_target="tpu_custom_call" | custom-call | tf_op jit(solution)/shard_map/unpack/pallas_call | solution.py:180
  220.7 3.0 %collective-permute-done.13 = f32[16,512]{1,0:T(8,128)S(1)} collective-permute-done((f32[16,512]{1,0:T(8,128)S(1)}, f32[16,512]{1,0:T(8,128)S(1)}, u32[]{:S(2)}, u32[]{:S(2)}) %collective-permute-start.13) | collective-permute-done | bytes 32800 | tf_op jit(solution)/shard_map/ppermute | solution.py:31
  (65 shorter events, 37.0 us)
Async XLA Ops:
  8.6 35.0 %all-to-all-start = ((bf16[16,16,512]{2,1,0:T(8,128)(2,1)}), bf16[16,16,512]{2,1,0:T(8,128)(2,1)S(1)}, u32[]{:S(2)}, u32[]{:S(2)}) async-start(bf16[16,16,512]{2,1,0:T(8,128)(2,1)} %broadcast_in_dim.2), calls=%async_computation | async-start | bytes 524288 | tf_op jit(solution)/shard_map/all_to_all | solution.py:197
  23.8 85.9 %all-gather.2.cloned.1.call-start = ((), (), s32[]{:S(2)}) async-start(), calls=%async_computation.2 | async-start | bytes 4456448 | tf_op jit(solution)/shard_map/all_gather | solution.py:206
  44.3 38.4 %collective-permute-start = (bf16[4,32,2048]{2,1,0:T(8,128)(2,1)S(1)}, bf16[4,32,2048]{2,1,0:T(8,128)(2,1)S(1)}, u32[]{:S(2)}, u32[]{:S(2)}) collective-permute-start(bf16[4,32,2048]{2,1,0:T(8,128)(2,1)S(1)} %get-tuple-element.37.p1), channel_id=1, source_target_pairs={{0,1},{1,2},{2,3},{3,0},{4,5},{5,6},{6,7},{7,4},{8,9},{9,10},{10,1... | collective-permute-start | bytes 1572872 | tf_op jit(solution)/shard_map/ppermute | solution.py:31
  48.7 41.7 %collective-permute-start.1 = (bf16[4,32,2048]{2,1,0:T(8,128)(2,1)S(1)}, bf16[4,32,2048]{2,1,0:T(8,128)(2,1)S(1)}, u32[]{:S(2)}, u32[]{:S(2)}) collective-permute-start(bf16[4,32,2048]{2,1,0:T(8,128)(2,1)S(1)} %get-tuple-element.38.p2), channel_id=1, source_target_pairs={{0,2},{1,3},{2,0},{3,1},{4,6},{5,7},{6,4},{7,5},{8,10},{9,11},{10,... | collective-permute-start | bytes 1572872 | tf_op jit(solution)/shard_map/ppermute | solution.py:31
  51.4 40.0 %collective-permute-start.2 = (bf16[4,32,2048]{2,1,0:T(8,128)(2,1)S(1)}, bf16[4,32,2048]{2,1,0:T(8,128)(2,1)S(1)}, u32[]{:S(2)}, u32[]{:S(2)}) collective-permute-start(bf16[4,32,2048]{2,1,0:T(8,128)(2,1)S(1)} %get-tuple-element.39.p3), channel_id=1, source_target_pairs={{0,3},{1,0},{2,1},{3,2},{4,7},{5,4},{6,5},{7,6},{8,11},{9,8},{10,9... | collective-permute-start | bytes 1572872 | tf_op jit(solution)/shard_map/ppermute | solution.py:31
  91.4 4.4 %copy-start.6 = (bf16[4,32,2048]{2,1,0:T(8,128)(2,1)}, bf16[4,32,2048]{2,1,0:T(8,128)(2,1)S(1)}, u32[]{:S(2)}) copy-start(bf16[4,32,2048]{2,1,0:T(8,128)(2,1)S(1)} %collective-permute-done.2.e3) | copy-start | bytes 1572868
  93.9 15.8 %collective-permute-start.3 = (bf16[128,2048]{1,0:T(8,128)(2,1)S(1)}, bf16[128,2048]{1,0:T(8,128)(2,1)S(1)}, u32[]{:S(2)}, u32[]{:S(2)}) collective-permute-start(bf16[128,2048]{1,0:T(8,128)(2,1)S(1)} %forward.1.a0), channel_id=1, source_target_pairs={{0,1},{1,2},{2,3},{3,0},{4,5},{5,6},{6,7},{7,4},{8,9},{9,10},{10,1... | collective-permute-start | bytes 1572872 | tf_op jit(solution)/shard_map/ppermute | solution.py:31
  109.7 9.3 %collective-permute-start.4 = (bf16[4,4,4,4,16,512]{5,4,3,2,1,0:T(8,128)(2,1)}, bf16[4,4,4,4,16,512]{5,4,3,2,1,0:T(8,128)(2,1)S(1)}, u32[]{:S(2)}, u32[]{:S(2)}) collective-permute-start(bf16[4,4,4,4,16,512]{5,4,3,2,1,0:T(8,128)(2,1)} %bitcast.20), channel_id=1, source_target_pairs={{0,4},{4,0},{1,5},{5,1},{2,6},{6,2},{3,7},{7,3},{8,12},{12,8},{9,1... | collective-permute-start | bytes 12582920 | tf_op jit(solution)/shard_map/ppermute | solution.py:214
  111.6 36.5 %collective-permute-start.5 = (bf16[128,2048]{1,0:T(8,128)(2,1)S(1)}, bf16[128,2048]{1,0:T(8,128)(2,1)S(1)}, u32[]{:S(2)}, u32[]{:S(2)}) collective-permute-start(bf16[128,2048]{1,0:T(8,128)(2,1)S(1)} %forward.1.a0), channel_id=1, source_target_pairs={{0,2},{1,3},{2,0},{3,1},{4,6},{5,7},{6,4},{7,5},{8,10},{9,11},{10,... | collective-permute-start | bytes 1572872 | tf_op jit(solution)/shard_map/ppermute | solution.py:31
  113.6 35.8 %collective-permute-start.6 = (bf16[128,2048]{1,0:T(8,128)(2,1)S(1)}, bf16[128,2048]{1,0:T(8,128)(2,1)S(1)}, u32[]{:S(2)}, u32[]{:S(2)}) collective-permute-start(bf16[128,2048]{1,0:T(8,128)(2,1)S(1)} %forward.1.a0), channel_id=1, source_target_pairs={{0,3},{1,0},{2,1},{3,2},{4,7},{5,4},{6,5},{7,6},{8,11},{9,8},{10,9... | collective-permute-start | bytes 1572872 | tf_op jit(solution)/shard_map/ppermute | solution.py:31
  123.3 8.5 %copy-start.2 = (bf16[4,4,4,4,16,512]{5,4,3,2,1,0:T(8,128)(2,1)}, bf16[4,4,4,4,16,512]{5,4,3,2,1,0:T(8,128)(2,1)S(1)}, u32[]{:S(2)}) copy-start(bf16[4,4,4,4,16,512]{5,4,3,2,1,0:T(8,128)(2,1)S(1)} %collective-permute-done.4.other_ref) | copy-start | bytes 12582916
  123.3 26.1 %copy-start.13 = (bf16[4,32,2048]{2,1,0:T(8,128)(2,1)S(1)}, bf16[4,32,2048]{2,1,0:T(8,128)(2,1)}, u32[]{:S(2)}) copy-start(bf16[4,32,2048]{2,1,0:T(8,128)(2,1)} %copy-done.12) | copy-start | bytes 1572868
  123.3 26.1 %copy-start.15 = (bf16[4,32,2048]{2,1,0:T(8,128)(2,1)S(1)}, bf16[4,32,2048]{2,1,0:T(8,128)(2,1)}, u32[]{:S(2)}) copy-start(bf16[4,32,2048]{2,1,0:T(8,128)(2,1)} %copy-done.14) | copy-start | bytes 1572868
  123.3 26.1 %copy-start.17 = (bf16[4,32,2048]{2,1,0:T(8,128)(2,1)S(1)}, bf16[4,32,2048]{2,1,0:T(8,128)(2,1)}, u32[]{:S(2)}) copy-start(bf16[4,32,2048]{2,1,0:T(8,128)(2,1)} %copy-done.16) | copy-start | bytes 1572868
  131.8 28.2 %copy-start.18 = (bf16[3,32,2048]{2,1,0:T(8,128)(2,1)}, bf16[3,32,2048]{2,1,0:T(8,128)(2,1)S(1)}, u32[]{:S(2)}) copy-start(bf16[3,32,2048]{2,1,0:T(8,128)(2,1)S(1)} %get-tuple-element.53) | copy-start | bytes 1179652
  131.8 28.2 %copy-start.19 = (bf16[3,32,2048]{2,1,0:T(8,128)(2,1)}, bf16[3,32,2048]{2,1,0:T(8,128)(2,1)S(1)}, u32[]{:S(2)}) copy-start(bf16[3,32,2048]{2,1,0:T(8,128)(2,1)S(1)} %get-tuple-element.52) | copy-start | bytes 1179652
  151.9 6.1 %collective-permute-start.7 = (f32[4,4,4,16,512]{4,3,2,1,0:T(8,128)S(1)}, f32[4,4,4,16,512]{4,3,2,1,0:T(8,128)S(1)}, u32[]{:S(2)}, u32[]{:S(2)}) collective-permute-start(f32[4,4,4,16,512]{4,3,2,1,0:T(8,128)S(1)} %get-tuple-element.49), channel_id=1, source_target_pairs={{0,4},{4,0},{1,5},{5,1},{2,6},{6,2},{3,7},{7,3},{8,12},{12,8},{9,1... | collective-permute-start | bytes 6291464 | tf_op jit(solution)/shard_map/ppermute | solution.py:242
  160.0 38.3 %all-to-all-start.1 = ((f32[16,4,16,512]{3,2,1,0:T(8,128)}), f32[16,4,16,512]{3,2,1,0:T(8,128)}, u32[]{:S(2)}, u32[]{:S(2)}) async-start(f32[16,4,16,512]{3,2,1,0:T(8,128)} %bitcast.23), calls=%async_computation.1 | async-start | bytes 4194304 | tf_op jit(solution)/shard_map/all_to_all | solution.py:243
  167.1 46.9 %collective-permute-start.10 = (bf16[3,32,2048]{2,1,0:T(8,128)(2,1)}, bf16[3,32,2048]{2,1,0:T(8,128)(2,1)S(1)}, u32[]{:S(2)}, u32[]{:S(2)}) collective-permute-start(bf16[3,32,2048]{2,1,0:T(8,128)(2,1)} %get-tuple-element.54), channel_id=1, source_target_pairs={{0,3},{1,0},{2,1},{3,2},{4,7},{5,4},{6,5},{7,6},{8,11},{9,8},{10,9... | collective-permute-start | bytes 1179656 | tf_op jit(solution)/shard_map/ppermute | solution.py:31
  169.0 48.0 %collective-permute-start.8 = (bf16[3,32,2048]{2,1,0:T(8,128)(2,1)}, bf16[3,32,2048]{2,1,0:T(8,128)(2,1)S(1)}, u32[]{:S(2)}, u32[]{:S(2)}) collective-permute-start(bf16[3,32,2048]{2,1,0:T(8,128)(2,1)} %copy-done.19), channel_id=1, source_target_pairs={{0,1},{1,2},{2,3},{3,0},{4,5},{5,6},{6,7},{7,4},{8,9},{9,10},{10,1... | collective-permute-start | bytes 1179656 | tf_op jit(solution)/shard_map/ppermute | solution.py:31
  172.9 44.1 %collective-permute-start.9 = (bf16[3,32,2048]{2,1,0:T(8,128)(2,1)}, bf16[3,32,2048]{2,1,0:T(8,128)(2,1)}, u32[]{:S(2)}, u32[]{:S(2)}) collective-permute-start(bf16[3,32,2048]{2,1,0:T(8,128)(2,1)} %copy-done.18), channel_id=1, source_target_pairs={{0,2},{1,3},{2,0},{3,1},{4,6},{5,7},{6,4},{7,5},{8,10},{9,11},{10,... | collective-permute-start | bytes 1179656 | tf_op jit(solution)/shard_map/ppermute | solution.py:31
  200.1 20.3 %collective-permute-start.11 = (f32[16,512]{1,0:T(8,128)S(1)}, f32[16,512]{1,0:T(8,128)S(1)}, u32[]{:S(2)}, u32[]{:S(2)}) collective-permute-start(f32[16,512]{1,0:T(8,128)S(1)} %get-tuple-element.59), channel_id=1, source_target_pairs={{0,32},{32,64},{64,96},{96,0},{1,33},{33,65},{65,97},{97,1},{2,34}... | collective-permute-start | bytes 98312 | tf_op jit(solution)/shard_map/ppermute | solution.py:31
  204.9 15.8 %collective-permute-start.12 = (f32[16,512]{1,0:T(8,128)S(1)}, f32[16,512]{1,0:T(8,128)S(1)}, u32[]{:S(2)}, u32[]{:S(2)}) collective-permute-start(f32[16,512]{1,0:T(8,128)S(1)} %get-tuple-element.61), channel_id=1, source_target_pairs={{0,64},{32,96},{64,0},{96,32},{1,65},{33,97},{65,1},{97,33},{2,66}... | collective-permute-start | bytes 98312 | tf_op jit(solution)/shard_map/ppermute | solution.py:31
  214.0 9.7 %collective-permute-start.13 = (f32[16,512]{1,0:T(8,128)S(1)}, f32[16,512]{1,0:T(8,128)S(1)}, u32[]{:S(2)}, u32[]{:S(2)}) collective-permute-start(f32[16,512]{1,0:T(8,128)S(1)} %get-tuple-element.60), channel_id=1, source_target_pairs={{0,96},{32,0},{64,32},{96,64},{1,97},{33,1},{65,33},{97,65},{2,98}... | collective-permute-start | bytes 98312 | tf_op jit(solution)/shard_map/ppermute | solution.py:31
  (14 other events, 19.5 us)
Sparse Core Ops, SparseCore 0:
  44.4 60.1 all-gather.1

commit v3 on v2

--- a/solution.py
+++ b/solution.py
@@ -201,8 +201,10 @@
         pack_kernel, "pack", [parcel] * 4, (pos, query_frames, key_frames, value_frames, out_grad), VMEM,
         [pltpu.VMEM((3, 4, 32, 2048), BF), pltpu.VMEM((16, 32, 512), BF), pltpu.VMEM((4, 4, 32, 512), F32), dma((4,))], 32,
     )
-    column, sent = lax.optimization_barrier((column, sent))
-    arrived = [sent[0]] + [shift(sent[n], "s", n) for n in (1, 2, 3)]
+    first = shift(sent[1], "s", 1)
+    column, two, three = lax.optimization_barrier((column, sent[2], sent[3]))
+    column, first = lax.optimization_barrier((column, first))
+    arrived = [sent[0], first, shift(two, "s", 2), shift(three, "s", 3)]
     mine = lax.all_gather(column.reshape(256, 512), ("x", "y"), axis=0, tiled=True).reshape(4, 4, 4, 4, 16, 512)
 
     attended = call(
@@ -210,7 +212,7 @@
         [pltpu.VMEM((3, 4, 32, 2048), BF), dma((4,))], 24,
     )
     attended_all = [attended] + [shift(attended, "s", n) for n in (1, 2, 3)]
-    mine, attended_all[1] = lax.optimization_barrier((mine, attended_all[1]))
+    mine, attended_all[2] = lax.optimization_barrier((mine, attended_all[2]))
     other = lax.ppermute(mine, "c", swap)
 
     back = call(

time: 232 us -> 230 us (level)
  waiting for transfers between devices: 102 us -> 85.9 us
  starting transfers between devices: 71.5 us -> 86.2 us
    ppermute x12, starting transfers between devices: 45.3 us -> 61.8 us  [shift(): return lax.ppermute(array, axis, [(i, (i + step) % 4) for i in range(4)])]
    ppermute x12, waiting for transfers between devices: 70.2 us -> 53.8 us  [shift(): return lax.ppermute(array, axis, [(i, (i + step) % 4) for i in range(4)])]
    all_gather x1, waiting for transfers between devices: 0.01 us -> 4.17 us  [per_device(): lax.all_gather(column.reshape(256, 512), ('x', 'y'), axis=0, tiled=True)]
    all_to_all x1, waiting for transfers between devices: 14.1 us -> 9.97 us  [per_device(): column = lax.all_to_all(spread, ('s', 'zh'), 0, 0)]
  transfers between devices with their start and end apart: 17 -> 17, of which waited for: 12 -> 11; matrix products, arithmetic and copies ran while one was open for 1% -> 1% of each run, Pallas kernels for 8% -> 8%
where the time goes in v3:
time: 230 us; the launch traced here: 229 us
  starting transfers between devices  86.2 us (37%)
  waiting for transfers between devices  85.9 us (37%)
  Pallas kernels  21.2 us (9%)
  local copies, waits for them, and re-layouts  16.8 us (7%)
  between operations  14.4 us (6%)
  other arithmetic  4.44 us (2%)
    ppermute x12, starting transfers between devices, shift(): return lax.ppermute(array, axis, [(i, (i + step) % 4) for i in range(4)])  61.8 us
    ppermute x12, waiting for transfers between devices, shift(): return lax.ppermute(array, axis, [(i, (i + step) % 4) for i in range(4)])  53.8 us
    pallas_call x6, Pallas kernels, call(): pl.pallas_call(kernel, out_shape=out_shape, in_specs=[SMEM] + [ANY] * (le...  21.2 us
    unnamed x42, local copies, waits for them, and re-layouts  15.2 us
    all_to_all x1, starting transfers between devices, per_device(): column = lax.all_to_all(spread, ('s', 'zh'), 0, 0)  15.2 us
    all_to_all x1, waiting for transfers between devices, per_device(): parts = lax.all_to_all(chip_sum.reshape(16, 4, 16, 512), ('x', 'y'), 0, 0)  12.4 us
    all_to_all x1, waiting for transfers between devices, per_device(): column = lax.all_to_all(spread, ('s', 'zh'), 0, 0)  9.97 us
    all_to_all x1, starting transfers between devices, per_device(): parts = lax.all_to_all(chip_sum.reshape(16, 4, 16, 512), ('x', 'y'), 0, 0)  5.3 us
  transfers between devices with their start and end apart: 17, of which 11 were waited for; matrix products, arithmetic and copies ran while one was open for 1% of the time, Pallas kernels for 8%

profile of v3, /device:TPU:32, one launch (start us, length us, event | category | flops | bytes accessed | tf_op | source)
XLA Modules:
  0.0 229.0 jit_solution(6326706127752194343)
XLA Ops:
  8.6 15.2 %all-to-all-start = ((bf16[16,16,512]{2,1,0:T(8,128)(2,1)}), bf16[16,16,512]{2,1,0:T(8,128)(2,1)S(1)}, u32[]{:S(2)}, u32[]{:S(2)}) async-start(bf16[16,16,512]{2,1,0:T(8,128)(2,1)} %broadcast_in_dim.2), calls=%async_computation | async-start | bytes 524288 | tf_op jit(solution)/shard_map/all_to_all | solution.py:197
  29.5 3.4 %collective-permute-start = (bf16[4,32,2048]{2,1,0:T(8,128)(2,1)S(1)}, bf16[4,32,2048]{2,1,0:T(8,128)(2,1)S(1)}, u32[]{:S(2)}, u32[]{:S(2)}) collective-permute-start(bf16[4,32,2048]{2,1,0:T(8,128)(2,1)S(1)} %get-tuple-element.36.p1), channel_id=1, source_target_pairs={{0,1},{1,2},{2,3},{3,0},{4,5},{5,6},{6,7},{7,4},{8,9},{9,10},{10,1... | collective-permute-start | bytes 1572872 | tf_op jit(solution)/shard_map/ppermute | solution.py:31
  33.7 10.0 %all-to-all-done = bf16[16,16,512]{2,1,0:T(8,128)(2,1)S(1)} async-done(((bf16[16,16,512]{2,1,0:T(8,128)(2,1)}), bf16[16,16,512]{2,1,0:T(8,128)(2,1)S(1)}, u32[]{:S(2)}, u32[]{:S(2)}) %all-to-all-start) | async-done | bytes 262176 | tf_op jit(solution)/shard_map/all_to_all | solution.py:197
  43.7 4.0 %collective-permute-done.e1 = bf16[4,32,2048]{2,1,0:T(8,128)(2,1)S(1)} collective-permute-done((bf16[4,32,2048]{2,1,0:T(8,128)(2,1)S(1)}, bf16[4,32,2048]{2,1,0:T(8,128)(2,1)S(1)}, u32[]{:S(2)}, u32[]{:S(2)}) %collective-permute-start) | collective-permute-done | bytes 524320 | tf_op jit(solution)/shard_map/ppermute | solution.py:31
  47.7 11.3 %collective-permute-start.1 = (bf16[4,32,2048]{2,1,0:T(8,128)(2,1)S(1)}, bf16[4,32,2048]{2,1,0:T(8,128)(2,1)S(1)}, u32[]{:S(2)}, u32[]{:S(2)}) collective-permute-start(bf16[4,32,2048]{2,1,0:T(8,128)(2,1)S(1)} %get-tuple-element.38.p2), channel_id=1, source_target_pairs={{0,2},{1,3},{2,0},{3,1},{4,6},{5,7},{6,4},{7,5},{8,10},{9,11},{10,... | collective-permute-start | bytes 1572872 | tf_op jit(solution)/shard_map/ppermute | solution.py:31
  59.8 3.6 %collective-permute-start.2 = (bf16[4,32,2048]{2,1,0:T(8,128)(2,1)S(1)}, bf16[4,32,2048]{2,1,0:T(8,128)(2,1)S(1)}, u32[]{:S(2)}, u32[]{:S(2)}) collective-permute-start(bf16[4,32,2048]{2,1,0:T(8,128)(2,1)S(1)} %get-tuple-element.39.p3), channel_id=1, source_target_pairs={{0,3},{1,0},{2,1},{3,2},{4,7},{5,4},{6,5},{7,6},{8,11},{9,8},{10,9... | collective-permute-start | bytes 1572872 | tf_op jit(solution)/shard_map/ppermute | solution.py:31
  64.2 20.9 %collective-permute-done.1.e2 = bf16[4,32,2048]{2,1,0:T(8,128)(2,1)S(1)} collective-permute-done((bf16[4,32,2048]{2,1,0:T(8,128)(2,1)S(1)}, bf16[4,32,2048]{2,1,0:T(8,128)(2,1)S(1)}, u32[]{:S(2)}, u32[]{:S(2)}) %collective-permute-start.1) | collective-permute-done | bytes 524320 | tf_op jit(solution)/shard_map/ppermute | solution.py:31
  89.0 3.9 %collective-permute-start.3 = (bf16[128,2048]{1,0:T(8,128)(2,1)S(1)}, bf16[128,2048]{1,0:T(8,128)(2,1)S(1)}, u32[]{:S(2)}, u32[]{:S(2)}) collective-permute-start(bf16[128,2048]{1,0:T(8,128)(2,1)S(1)} %forward.1.a0), channel_id=1, source_target_pairs={{0,2},{1,3},{2,0},{3,1},{4,6},{5,7},{6,4},{7,5},{8,10},{9,11},{10,... | collective-permute-start | bytes 1572872 | tf_op jit(solution)/shard_map/ppermute | solution.py:31
  92.9 18.9 %collective-permute-done.3.a2 = bf16[128,2048]{1,0:T(8,128)(2,1)S(1)} collective-permute-done((bf16[128,2048]{1,0:T(8,128)(2,1)S(1)}, bf16[128,2048]{1,0:T(8,128)(2,1)S(1)}, u32[]{:S(2)}, u32[]{:S(2)}) %collective-permute-start.3) | collective-permute-done | bytes 524320 | tf_op jit(solution)/shard_map/ppermute | solution.py:31
  111.8 4.2 %all-gather.2.cloned.1.call-done = bf16[4096,512]{1,0:T(8,128)(2,1)} async-done(((bf16[256,512]{1,0:T(8,128)(2,1)}), bf16[4096,512]{1,0:T(8,128)(2,1)}) %all-gather.2.cloned.1.call-update) | async-done | bytes 4194320 | tf_op jit(solution)/shard_map/all_gather | solution.py:208
  117.9 3.5 %collective-permute-start.5 = (bf16[128,2048]{1,0:T(8,128)(2,1)S(1)}, bf16[128,2048]{1,0:T(8,128)(2,1)S(1)}, u32[]{:S(2)}, u32[]{:S(2)}) collective-permute-start(bf16[128,2048]{1,0:T(8,128)(2,1)S(1)} %forward.1.a0), channel_id=1, source_target_pairs={{0,1},{1,2},{2,3},{3,0},{4,5},{5,6},{6,7},{7,4},{8,9},{9,10},{10,1... | collective-permute-start | bytes 1572872 | tf_op jit(solution)/shard_map/ppermute | solution.py:31
  129.5 8.5 %backward.1 = (bf16[3,32,2048]{2,1,0:T(8,128)(2,1)S(1)}, bf16[3,32,2048]{2,1,0:T(8,128)(2,1)S(1)}, bf16[3,32,2048]{2,1,0:T(8,128)(2,1)S(1)}, bf16[3,32,2048]{2,1,0:T(8,128)(2,1)}) custom-call(s32[5]{0:T(128)S(1)} %stack.23.pos_ref, bf16[4,32,2048]{2,1,0:T(8,128)(2,1)S(1)} %get-tuple-element.32.e0.p0, bf16[4,32,2048]{2,1,0:T(8,128)(2,1)S(1)} %collective-permute-done.e1, ...), custom_call_target="tpu_custom_call" | custom-call | tf_op jit(solution)/shard_map/backward/pallas_call | solution.py:180
  138.0 8.1 %collective-permute-done.6.a3 = bf16[128,2048]{1,0:T(8,128)(2,1)S(1)} collective-permute-done((bf16[128,2048]{1,0:T(8,128)(2,1)S(1)}, bf16[128,2048]{1,0:T(8,128)(2,1)S(1)}, u32[]{:S(2)}, u32[]{:S(2)}) %collective-permute-start.6) | collective-permute-done | bytes 524320 | tf_op jit(solution)/shard_map/ppermute | solution.py:31
  146.2 2.5 %weight.1 = (f32[4,4,4,16,512]{4,3,2,1,0:T(8,128)S(1)}, f32[4,4,4,16,512]{4,3,2,1,0:T(8,128)S(1)}) custom-call(s32[5]{0:T(128)S(1)} %stack.23.pos_ref, bf16[128,2048]{1,0:T(8,128)(2,1)S(1)} %forward.1.a0, bf16[128,2048]{1,0:T(8,128)(2,1)S(1)} %collective-permute-done.5.a1, bf16[128,2048]{1,0:T(8,128)(2,1)S(1)} %collective-permute-done.3.a2, ...), custom_call_target="tpu_custom_call" | custom-call | tf_op jit(solution)/shard_map/weight/pallas_call | solution.py:180
  150.6 4.1 %collective-permute-done.7 = f32[4,4,4,16,512]{4,3,2,1,0:T(8,128)S(1)} collective-permute-done((f32[4,4,4,16,512]{4,3,2,1,0:T(8,128)S(1)}, f32[4,4,4,16,512]{4,3,2,1,0:T(8,128)S(1)}, u32[]{:S(2)}, u32[]{:S(2)}) %collective-permute-start.7) | collective-permute-done | bytes 2097184 | tf_op jit(solution)/shard_map/ppermute | solution.py:244
  156.8 5.3 %all-to-all-start.1 = ((f32[16,4,16,512]{3,2,1,0:T(8,128)}), f32[16,4,16,512]{3,2,1,0:T(8,128)}, u32[]{:S(2)}, u32[]{:S(2)}) async-start(f32[16,4,16,512]{3,2,1,0:T(8,128)} %bitcast.23), calls=%async_computation.1 | async-start | bytes 4194304 | tf_op jit(solution)/shard_map/all_to_all | solution.py:245
  162.1 3.4 %collective-permute-start.10 = (bf16[3,32,2048]{2,1,0:T(8,128)(2,1)}, bf16[3,32,2048]{2,1,0:T(8,128)(2,1)S(1)}, u32[]{:S(2)}, u32[]{:S(2)}) collective-permute-start(bf16[3,32,2048]{2,1,0:T(8,128)(2,1)} %get-tuple-element.54), channel_id=1, source_target_pairs={{0,3},{1,0},{2,1},{3,2},{4,7},{5,4},{6,5},{7,6},{8,11},{9,8},{10,9... | collective-permute-start | bytes 1179656 | tf_op jit(solution)/shard_map/ppermute | solution.py:31
  167.9 5.5 %collective-permute-start.9 = (bf16[3,32,2048]{2,1,0:T(8,128)(2,1)}, bf16[3,32,2048]{2,1,0:T(8,128)(2,1)}, u32[]{:S(2)}, u32[]{:S(2)}) collective-permute-start(bf16[3,32,2048]{2,1,0:T(8,128)(2,1)} %copy-done.18), channel_id=1, source_target_pairs={{0,2},{1,3},{2,0},{3,1},{4,6},{5,7},{6,4},{7,5},{8,10},{9,11},{10,... | collective-permute-start | bytes 1179656 | tf_op jit(solution)/shard_map/ppermute | solution.py:31
  177.8 3.1 %project.1 = bf16[16,32,512]{2,1,0:T(8,128)(2,1)} custom-call(s32[5]{0:T(128)S(1)} %stack.23.pos_ref, bf16[128,2048]{1,0:T(8,128)(2,1)S(1)} %forward.1.a0, bf16[128,2048]{1,0:T(8,128)(2,1)S(1)} %collective-permute-done.5.a1, bf16[128,2048]{1,0:T(8,128)(2,1)S(1)} %collective-permute-done.3.a2, bf16[128,2048]{1,0:T(8,128)(2,1)S(1)} %collective-permute-done.6.a3, ...), custom_call_target="tpu_custom_call" | custom-call | tf_op jit(solution)/shard_map/project/pallas_call | solution.py:180
  180.9 12.4 %all-to-all-done.1 = f32[16,4,16,512]{3,2,1,0:T(8,128)} async-done(((f32[16,4,16,512]{3,2,1,0:T(8,128)}), f32[16,4,16,512]{3,2,1,0:T(8,128)}, u32[]{:S(2)}, u32[]{:S(2)}) %all-to-all-start.1) | async-done | bytes 2097184 | tf_op jit(solution)/shard_map/all_to_all | solution.py:245
  195.1 7.6 %collective-permute-start.11 = (f32[16,512]{1,0:T(8,128)S(1)}, f32[16,512]{1,0:T(8,128)S(1)}, u32[]{:S(2)}, u32[]{:S(2)}) collective-permute-start(f32[16,512]{1,0:T(8,128)S(1)} %get-tuple-element.59), channel_id=1, source_target_pairs={{0,32},{32,64},{64,96},{96,0},{1,33},{33,65},{65,97},{97,1},{2,34}... | collective-permute-start | bytes 98312 | tf_op jit(solution)/shard_map/ppermute | solution.py:31
  202.7 8.0 %collective-permute-start.12 = (f32[16,512]{1,0:T(8,128)S(1)}, f32[16,512]{1,0:T(8,128)S(1)}, u32[]{:S(2)}, u32[]{:S(2)}) collective-permute-start(f32[16,512]{1,0:T(8,128)S(1)} %get-tuple-element.61), channel_id=1, source_target_pairs={{0,64},{32,96},{64,0},{96,32},{1,65},{33,97},{65,1},{97,33},{2,66}... | collective-permute-start | bytes 98312 | tf_op jit(solution)/shard_map/ppermute | solution.py:31
  210.7 6.9 %collective-permute-start.13 = (f32[16,512]{1,0:T(8,128)S(1)}, f32[16,512]{1,0:T(8,128)S(1)}, u32[]{:S(2)}, u32[]{:S(2)}) collective-permute-start(f32[16,512]{1,0:T(8,128)S(1)} %get-tuple-element.60), channel_id=1, source_target_pairs={{0,96},{32,0},{64,32},{96,64},{1,97},{33,1},{65,33},{97,65},{2,98}... | collective-permute-start | bytes 98312 | tf_op jit(solution)/shard_map/ppermute | solution.py:31
  217.7 3.4 %unpack.1 = (bf16[4,32,2048]{2,1,0:T(8,128)(2,1)}, bf16[4,32,2048]{2,1,0:T(8,128)(2,1)}, bf16[4,32,2048]{2,1,0:T(8,128)(2,1)}) custom-call(s32[5]{0:T(128)S(1)} %stack.23.pos_ref, bf16[3,32,2048]{2,1,0:T(8,128)(2,1)S(1)} %get-tuple-element.51.h0, bf16[3,32,2048]{2,1,0:T(8,128)(2,1)S(1)} %collective-permute-done.8.h1, ...), custom_call_target="tpu_custom_call" | custom-call | tf_op jit(solution)/shard_map/unpack/pallas_call | solution.py:180
  (65 shorter events, 37.1 us)
Async XLA Ops:
  8.6 35.0 %all-to-all-start = ((bf16[16,16,512]{2,1,0:T(8,128)(2,1)}), bf16[16,16,512]{2,1,0:T(8,128)(2,1)S(1)}, u32[]{:S(2)}, u32[]{:S(2)}) async-start(bf16[16,16,512]{2,1,0:T(8,128)(2,1)} %broadcast_in_dim.2), calls=%async_computation | async-start | bytes 524288 | tf_op jit(solution)/shard_map/all_to_all | solution.py:197
  23.8 92.1 %all-gather.2.cloned.1.call-start = ((), (), s32[]{:S(2)}) async-start(), calls=%async_computation.2 | async-start | bytes 4456448 | tf_op jit(solution)/shard_map/all_gather | solution.py:208
  29.5 18.2 %collective-permute-start = (bf16[4,32,2048]{2,1,0:T(8,128)(2,1)S(1)}, bf16[4,32,2048]{2,1,0:T(8,128)(2,1)S(1)}, u32[]{:S(2)}, u32[]{:S(2)}) collective-permute-start(bf16[4,32,2048]{2,1,0:T(8,128)(2,1)S(1)} %get-tuple-element.36.p1), channel_id=1, source_target_pairs={{0,1},{1,2},{2,3},{3,0},{4,5},{5,6},{6,7},{7,4},{8,9},{9,10},{10,1... | collective-permute-start | bytes 1572872 | tf_op jit(solution)/shard_map/ppermute | solution.py:31
  47.7 37.4 %collective-permute-start.1 = (bf16[4,32,2048]{2,1,0:T(8,128)(2,1)S(1)}, bf16[4,32,2048]{2,1,0:T(8,128)(2,1)S(1)}, u32[]{:S(2)}, u32[]{:S(2)}) collective-permute-start(bf16[4,32,2048]{2,1,0:T(8,128)(2,1)S(1)} %get-tuple-element.38.p2), channel_id=1, source_target_pairs={{0,2},{1,3},{2,0},{3,1},{4,6},{5,7},{6,4},{7,5},{8,10},{9,11},{10,... | collective-permute-start | bytes 1572872 | tf_op jit(solution)/shard_map/ppermute | solution.py:31
  59.8 26.8 %collective-permute-start.2 = (bf16[4,32,2048]{2,1,0:T(8,128)(2,1)S(1)}, bf16[4,32,2048]{2,1,0:T(8,128)(2,1)S(1)}, u32[]{:S(2)}, u32[]{:S(2)}) collective-permute-start(bf16[4,32,2048]{2,1,0:T(8,128)(2,1)S(1)} %get-tuple-element.39.p3), channel_id=1, source_target_pairs={{0,3},{1,0},{2,1},{3,2},{4,7},{5,4},{6,5},{7,6},{8,11},{9,8},{10,9... | collective-permute-start | bytes 1572872 | tf_op jit(solution)/shard_map/ppermute | solution.py:31
  86.6 6.3 %copy-start.6 = (bf16[4,32,2048]{2,1,0:T(8,128)(2,1)}, bf16[4,32,2048]{2,1,0:T(8,128)(2,1)S(1)}, u32[]{:S(2)}) copy-start(bf16[4,32,2048]{2,1,0:T(8,128)(2,1)S(1)} %collective-permute-done.2.e3) | copy-start | bytes 1572868
  89.0 22.8 %collective-permute-start.3 = (bf16[128,2048]{1,0:T(8,128)(2,1)S(1)}, bf16[128,2048]{1,0:T(8,128)(2,1)S(1)}, u32[]{:S(2)}, u32[]{:S(2)}) collective-permute-start(bf16[128,2048]{1,0:T(8,128)(2,1)S(1)} %forward.1.a0), channel_id=1, source_target_pairs={{0,2},{1,3},{2,0},{3,1},{4,6},{5,7},{6,4},{7,5},{8,10},{9,11},{10,... | collective-permute-start | bytes 1572872 | tf_op jit(solution)/shard_map/ppermute | solution.py:31
  116.0 9.3 %collective-permute-start.4 = (bf16[4,4,4,4,16,512]{5,4,3,2,1,0:T(8,128)(2,1)}, bf16[4,4,4,4,16,512]{5,4,3,2,1,0:T(8,128)(2,1)S(1)}, u32[]{:S(2)}, u32[]{:S(2)}) collective-permute-start(bf16[4,4,4,4,16,512]{5,4,3,2,1,0:T(8,128)(2,1)} %bitcast.20), channel_id=1, source_target_pairs={{0,4},{4,0},{1,5},{5,1},{2,6},{6,2},{3,7},{7,3},{8,12},{12,8},{9,1... | collective-permute-start | bytes 12582920 | tf_op jit(solution)/shard_map/ppermute | solution.py:216
  117.9 20.2 %collective-permute-start.5 = (bf16[128,2048]{1,0:T(8,128)(2,1)S(1)}, bf16[128,2048]{1,0:T(8,128)(2,1)S(1)}, u32[]{:S(2)}, u32[]{:S(2)}) collective-permute-start(bf16[128,2048]{1,0:T(8,128)(2,1)S(1)} %forward.1.a0), channel_id=1, source_target_pairs={{0,1},{1,2},{2,3},{3,0},{4,5},{5,6},{6,7},{7,4},{8,9},{9,10},{10,1... | collective-permute-start | bytes 1572872 | tf_op jit(solution)/shard_map/ppermute | solution.py:31
  121.3 24.8 %collective-permute-start.6 = (bf16[128,2048]{1,0:T(8,128)(2,1)S(1)}, bf16[128,2048]{1,0:T(8,128)(2,1)S(1)}, u32[]{:S(2)}, u32[]{:S(2)}) collective-permute-start(bf16[128,2048]{1,0:T(8,128)(2,1)S(1)} %forward.1.a0), channel_id=1, source_target_pairs={{0,3},{1,0},{2,1},{3,2},{4,7},{5,4},{6,5},{7,6},{8,11},{9,8},{10,9... | collective-permute-start | bytes 1572872 | tf_op jit(solution)/shard_map/ppermute | solution.py:31
  129.5 8.5 %copy-start.2 = (bf16[4,4,4,4,16,512]{5,4,3,2,1,0:T(8,128)(2,1)}, bf16[4,4,4,4,16,512]{5,4,3,2,1,0:T(8,128)(2,1)S(1)}, u32[]{:S(2)}) copy-start(bf16[4,4,4,4,16,512]{5,4,3,2,1,0:T(8,128)(2,1)S(1)} %collective-permute-done.4.other_ref) | copy-start | bytes 12582916
  129.5 16.7 %copy-start.13 = (bf16[4,32,2048]{2,1,0:T(8,128)(2,1)S(1)}, bf16[4,32,2048]{2,1,0:T(8,128)(2,1)}, u32[]{:S(2)}) copy-start(bf16[4,32,2048]{2,1,0:T(8,128)(2,1)} %copy-done.12) | copy-start | bytes 1572868
  129.5 16.7 %copy-start.15 = (bf16[4,32,2048]{2,1,0:T(8,128)(2,1)S(1)}, bf16[4,32,2048]{2,1,0:T(8,128)(2,1)}, u32[]{:S(2)}) copy-start(bf16[4,32,2048]{2,1,0:T(8,128)(2,1)} %copy-done.14) | copy-start | bytes 1572868
  129.5 16.7 %copy-start.17 = (bf16[4,32,2048]{2,1,0:T(8,128)(2,1)S(1)}, bf16[4,32,2048]{2,1,0:T(8,128)(2,1)}, u32[]{:S(2)}) copy-start(bf16[4,32,2048]{2,1,0:T(8,128)(2,1)} %copy-done.16) | copy-start | bytes 1572868
  138.0 18.7 %copy-start.18 = (bf16[3,32,2048]{2,1,0:T(8,128)(2,1)}, bf16[3,32,2048]{2,1,0:T(8,128)(2,1)S(1)}, u32[]{:S(2)}) copy-start(bf16[3,32,2048]{2,1,0:T(8,128)(2,1)S(1)} %get-tuple-element.53) | copy-start | bytes 1179652
  138.0 18.7 %copy-start.19 = (bf16[3,32,2048]{2,1,0:T(8,128)(2,1)}, bf16[3,32,2048]{2,1,0:T(8,128)(2,1)S(1)}, u32[]{:S(2)}) copy-start(bf16[3,32,2048]{2,1,0:T(8,128)(2,1)S(1)} %get-tuple-element.52) | copy-start | bytes 1179652
  148.6 6.1 %collective-permute-start.7 = (f32[4,4,4,16,512]{4,3,2,1,0:T(8,128)S(1)}, f32[4,4,4,16,512]{4,3,2,1,0:T(8,128)S(1)}, u32[]{:S(2)}, u32[]{:S(2)}) collective-permute-start(f32[4,4,4,16,512]{4,3,2,1,0:T(8,128)S(1)} %get-tuple-element.49), channel_id=1, source_target_pairs={{0,4},{4,0},{1,5},{5,1},{2,6},{6,2},{3,7},{7,3},{8,12},{12,8},{9,1... | collective-permute-start | bytes 6291464 | tf_op jit(solution)/shard_map/ppermute | solution.py:244
  156.8 36.5 %all-to-all-start.1 = ((f32[16,4,16,512]{3,2,1,0:T(8,128)}), f32[16,4,16,512]{3,2,1,0:T(8,128)}, u32[]{:S(2)}, u32[]{:S(2)}) async-start(f32[16,4,16,512]{3,2,1,0:T(8,128)} %bitcast.23), calls=%async_computation.1 | async-start | bytes 4194304 | tf_op jit(solution)/shard_map/all_to_all | solution.py:245
  162.1 48.7 %collective-permute-start.10 = (bf16[3,32,2048]{2,1,0:T(8,128)(2,1)}, bf16[3,32,2048]{2,1,0:T(8,128)(2,1)S(1)}, u32[]{:S(2)}, u32[]{:S(2)}) collective-permute-start(bf16[3,32,2048]{2,1,0:T(8,128)(2,1)} %get-tuple-element.54), channel_id=1, source_target_pairs={{0,3},{1,0},{2,1},{3,2},{4,7},{5,4},{6,5},{7,6},{8,11},{9,8},{10,9... | collective-permute-start | bytes 1179656 | tf_op jit(solution)/shard_map/ppermute | solution.py:31
  165.4 52.2 %collective-permute-start.8 = (bf16[3,32,2048]{2,1,0:T(8,128)(2,1)}, bf16[3,32,2048]{2,1,0:T(8,128)(2,1)S(1)}, u32[]{:S(2)}, u32[]{:S(2)}) collective-permute-start(bf16[3,32,2048]{2,1,0:T(8,128)(2,1)} %copy-done.19), channel_id=1, source_target_pairs={{0,1},{1,2},{2,3},{3,0},{4,5},{5,6},{6,7},{7,4},{8,9},{9,10},{10,1... | collective-permute-start | bytes 1179656 | tf_op jit(solution)/shard_map/ppermute | solution.py:31
  167.9 49.8 %collective-permute-start.9 = (bf16[3,32,2048]{2,1,0:T(8,128)(2,1)}, bf16[3,32,2048]{2,1,0:T(8,128)(2,1)}, u32[]{:S(2)}, u32[]{:S(2)}) collective-permute-start(bf16[3,32,2048]{2,1,0:T(8,128)(2,1)} %copy-done.18), channel_id=1, source_target_pairs={{0,2},{1,3},{2,0},{3,1},{4,6},{5,7},{6,4},{7,5},{8,10},{9,11},{10,... | collective-permute-start | bytes 1179656 | tf_op jit(solution)/shard_map/ppermute | solution.py:31
  195.1 26.0 %collective-permute-start.11 = (f32[16,512]{1,0:T(8,128)S(1)}, f32[16,512]{1,0:T(8,128)S(1)}, u32[]{:S(2)}, u32[]{:S(2)}) collective-permute-start(f32[16,512]{1,0:T(8,128)S(1)} %get-tuple-element.59), channel_id=1, source_target_pairs={{0,32},{32,64},{64,96},{96,0},{1,33},{33,65},{65,97},{97,1},{2,34}... | collective-permute-start | bytes 98312 | tf_op jit(solution)/shard_map/ppermute | solution.py:31
  202.7 18.4 %collective-permute-start.12 = (f32[16,512]{1,0:T(8,128)S(1)}, f32[16,512]{1,0:T(8,128)S(1)}, u32[]{:S(2)}, u32[]{:S(2)}) collective-permute-start(f32[16,512]{1,0:T(8,128)S(1)} %get-tuple-element.61), channel_id=1, source_target_pairs={{0,64},{32,96},{64,0},{96,32},{1,65},{33,97},{65,1},{97,33},{2,66}... | collective-permute-start | bytes 98312 | tf_op jit(solution)/shard_map/ppermute | solution.py:31
  210.7 10.8 %collective-permute-start.13 = (f32[16,512]{1,0:T(8,128)S(1)}, f32[16,512]{1,0:T(8,128)S(1)}, u32[]{:S(2)}, u32[]{:S(2)}) collective-permute-start(f32[16,512]{1,0:T(8,128)S(1)} %get-tuple-element.60), channel_id=1, source_target_pairs={{0,96},{32,0},{64,32},{96,64},{1,97},{33,1},{65,33},{97,65},{2,98}... | collective-permute-start | bytes 98312 | tf_op jit(solution)/shard_map/ppermute | solution.py:31
  (14 other events, 23.1 us)
Sparse Core Ops, SparseCore 0:
  47.8 68.0 all-gather.1

commit v4 on v3

--- a/solution.py
+++ b/solution.py
@@ -51,7 +51,9 @@
         copy.wait()
 
 
-def pack_kernel(pos_ref, q_ref, k_ref, v_ref, g_ref, o0, o1, o2, o3, rows_ref, grad_ref, wide_ref, sems):
+def pack_kernel(
+    pos_ref, q_ref, k_ref, v_ref, g_ref, o0, o1, o2, o3, stay_ref, rows_ref, grad_ref, wide_ref, sems
+):
     pairs = [(ref, rows_ref.at[which]) for which, ref in enumerate((q_ref, k_ref, v_ref))]
     copies = run_copies(pairs + [(g_ref, grad_ref)], sems)
     for which in range(4):
@@ -62,7 +64,10 @@
             wide_ref[part] = block.astype(F32)
             for step, out in enumerate((o0, o1, o2, o3)):
                 pixels = pl.ds(pl.multiple_of(wrap(pos_ref[S], step) * 8, 8), 8)
-                out[which, :, lanes] = wide_ref[part, :, pixels, :].reshape(32, 512).astype(BF)
+                rows = wide_ref[part, :, pixels, :].reshape(32, 512).astype(BF)
+                out[which, :, lanes] = rows
+                if which == 3:
+                    stay_ref[step, part] = rows
 
 
 def unpack_kernel(pos_ref, h0, h1, h2, h3, q_ref, k_ref, v_ref, rows_ref, wide_ref, sems):
@@ -148,10 +153,9 @@
     wait_all(run_copies(pairs, out_sems))
 
 
-def weight_kernel(pos_ref, a0, a1, a2, a3, p0, p1, p2, p3, keep_ref, send_ref, att_ref, grad_ref, sum_ref, sems):
+def weight_kernel(pos_ref, a0, a1, a2, a3, stay_ref, keep_ref, send_ref, att_ref, grad_ref, sum_ref, sems):
     pairs = [(ref, att_ref.at[step]) for step, ref in enumerate((a0, a1, a2, a3))]
-    for step, ref in enumerate((p0, p3, p2, p1)):
-        pairs += [(ref.at[3, :, 512 * g : 512 * g + 512], grad_ref.at[step, g]) for g in range(4)]
+    pairs += [(stay_ref.at[(4 - step) % 4], grad_ref.at[step]) for step in range(4)]
     wait_all(run_copies(pairs, sems))
     grads = grad_ref[...].reshape(512, 512)
     c = pos_ref[C]
@@ -197,8 +201,8 @@
     column = lax.all_to_all(spread, ("s", "zh"), 0, 0)
 
     parcel = jax.ShapeDtypeStruct((4, 32, 2048), BF)
-    sent = call(
-        pack_kernel, "pack", [parcel] * 4, (pos, query_frames, key_frames, value_frames, out_grad), VMEM,
+    *sent, stay = call(
+        pack_kernel, "pack", [parcel] * 4 + [jax.ShapeDtypeStruct((4, 4, 32, 512), BF)], (pos, query_frames, key_frames, value_frames, out_grad), VMEM,
         [pltpu.VMEM((3, 4, 32, 2048), BF), pltpu.VMEM((16, 32, 512), BF), pltpu.VMEM((4, 4, 32, 512), F32), dma((4,))], 32,
     )
     first = shift(sent[1], "s", 1)
@@ -232,7 +236,7 @@
 
     quarter = jax.ShapeDtypeStruct((4, 4, 4, 16, 512), F32)
     keep, send = call(
-        weight_kernel, "weight", [quarter] * 2, (pos, *attended_all, *sent), VMEM,
+        weight_kernel, "weight", [quarter] * 2, (pos, *attended_all, stay), VMEM,
         [
             pltpu.VMEM((4, 128, 2048), BF),
             pltpu.VMEM((4, 4, 32, 512), BF),
@@ -260,11 +264,7 @@
     )
     parts, block_out = lax.optimization_barrier((parts, block_out))
     plane_sum = parts.sum(axis=0)
-    weight_grad = None
-    for step in range(4):
-        part = lax.dynamic_index_in_dim(plane_sum, wrap(pos[ZH], step), 0, keepdims=False)
-        got = part if step == 0 else shift(part, "zh", step)
-        weight_grad = got if weight_grad is None else weight_grad + got
+    weight_grad = lax.all_to_all(plane_sum, "zh", 0, 0).sum(axis=0)
     return block_out, query_grad, key_grad, value_grad, weight_grad
 
 

time: 230 us -> 231 us (level)
  waiting for transfers between devices: 85.9 us -> 98.4 us
  starting transfers between devices: 86.2 us -> 75.2 us
    ppermute x12 -> x9, starting transfers between devices: 61.8 us -> 38.6 us  [shift(): return lax.ppermute(array, axis, [(i, (i + step) % 4) for i in range(4)])]
    all_to_all x0 -> x1, starting transfers between devices: none -> 11.1 us  [per_device(): weight_grad = lax.all_to_all(plane_sum, 'zh', 0, 0).sum(axis=0)]
    all_to_all x0 -> x1, waiting for transfers between devices: none -> 10.7 us  [per_device(): weight_grad = lax.all_to_all(plane_sum, 'zh', 0, 0).sum(axis=0)]
    ppermute x12 -> x9, waiting for transfers between devices: 53.8 us -> 58.1 us  [shift(): return lax.ppermute(array, axis, [(i, (i + step) % 4) for i in range(4)])]
    all_gather x1, waiting for transfers between devices: 4.17 us -> 1.61 us  [per_device(): lax.all_gather(column.reshape(256, 512), ('x', 'y'), axis=0, tiled=True)]
    unnamed x42 -> x34, local copies, waits for them, and re-layouts: 15.2 us -> 13.6 us
  transfers between devices with their start and end apart: 17 -> 15, of which waited for: 11 -> 11; matrix products, arithmetic and copies ran while one was open for 1% -> 1% of each run, Pallas kernels for 8% -> 8%
where the time goes in v4:
time: 231 us; the launch traced here: 230 us
  waiting for transfers between devices  98.4 us (43%)
  starting transfers between devices  75.2 us (33%)
  Pallas kernels  21.8 us (9%)
  local copies, waits for them, and re-layouts  15.2 us (7%)
  between operations  14.3 us (6%)
  other arithmetic  5.09 us (2%)
    ppermute x9, waiting for transfers between devices, shift(): return lax.ppermute(array, axis, [(i, (i + step) % 4) for i in range(4)])  58.1 us
    ppermute x9, starting transfers between devices, shift(): return lax.ppermute(array, axis, [(i, (i + step) % 4) for i in range(4)])  38.6 us
    pallas_call x6, Pallas kernels, call(): pl.pallas_call(kernel, out_shape=out_shape, in_specs=[SMEM] + [ANY] * (le...  21.8 us
    all_to_all x1, starting transfers between devices, per_device(): column = lax.all_to_all(spread, ('s', 'zh'), 0, 0)  15.2 us
    unnamed x34, local copies, waits for them, and re-layouts  13.6 us
    all_to_all x1, waiting for transfers between devices, per_device(): parts = lax.all_to_all(chip_sum.reshape(16, 4, 16, 512), ('x', 'y'), 0, 0)  12.5 us
    all_to_all x1, starting transfers between devices, per_device(): weight_grad = lax.all_to_all(plane_sum, 'zh', 0, 0).sum(axis=0)  11.1 us
    all_to_all x1, waiting for transfers between devices, per_device(): weight_grad = lax.all_to_all(plane_sum, 'zh', 0, 0).sum(axis=0)  10.7 us
  transfers between devices with their start and end apart: 15, of which 11 were waited for; matrix products, arithmetic and copies ran while one was open for 1% of the time, Pallas kernels for 8%

profile of v4, /device:TPU:32, one launch (start us, length us, event | category | flops | bytes accessed | tf_op | source)
XLA Modules:
  0.0 229.9 jit_solution(6979410867991033402)
XLA Ops:
  8.6 15.2 %all-to-all-start = ((bf16[16,16,512]{2,1,0:T(8,128)(2,1)}), bf16[16,16,512]{2,1,0:T(8,128)(2,1)S(1)}, u32[]{:S(2)}, u32[]{:S(2)}) async-start(bf16[16,16,512]{2,1,0:T(8,128)(2,1)} %broadcast_in_dim.2), calls=%async_computation | async-start | bytes 524288 | tf_op jit(solution)/shard_map/all_to_all | solution.py:201
  30.3 3.4 %collective-permute-start = (bf16[4,32,2048]{2,1,0:T(8,128)(2,1)S(1)}, bf16[4,32,2048]{2,1,0:T(8,128)(2,1)S(1)}, u32[]{:S(2)}, u32[]{:S(2)}) collective-permute-start(bf16[4,32,2048]{2,1,0:T(8,128)(2,1)S(1)} %get-tuple-element.37), channel_id=1, source_target_pairs={{0,1},{1,2},{2,3},{3,0},{4,5},{5,6},{6,7},{7,4},{8,9},{9,10},{10,1... | collective-permute-start | bytes 1572872 | tf_op jit(solution)/shard_map/ppermute | solution.py:31
  33.7 10.0 %all-to-all-done = bf16[16,16,512]{2,1,0:T(8,128)(2,1)S(1)} async-done(((bf16[16,16,512]{2,1,0:T(8,128)(2,1)}), bf16[16,16,512]{2,1,0:T(8,128)(2,1)S(1)}, u32[]{:S(2)}, u32[]{:S(2)}) %all-to-all-start) | async-done | bytes 262176 | tf_op jit(solution)/shard_map/all_to_all | solution.py:201
  43.7 4.2 %collective-permute-done.e1 = bf16[4,32,2048]{2,1,0:T(8,128)(2,1)S(1)} collective-permute-done((bf16[4,32,2048]{2,1,0:T(8,128)(2,1)S(1)}, bf16[4,32,2048]{2,1,0:T(8,128)(2,1)S(1)}, u32[]{:S(2)}, u32[]{:S(2)}) %collective-permute-start) | collective-permute-done | bytes 524320 | tf_op jit(solution)/shard_map/ppermute | solution.py:31
  47.9 3.6 %collective-permute-start.1 = (bf16[4,32,2048]{2,1,0:T(8,128)(2,1)S(1)}, bf16[4,32,2048]{2,1,0:T(8,128)(2,1)S(1)}, u32[]{:S(2)}, u32[]{:S(2)}) collective-permute-start(bf16[4,32,2048]{2,1,0:T(8,128)(2,1)S(1)} %get-tuple-element.39), channel_id=1, source_target_pairs={{0,2},{1,3},{2,0},{3,1},{4,6},{5,7},{6,4},{7,5},{8,10},{9,11},{10,... | collective-permute-start | bytes 1572872 | tf_op jit(solution)/shard_map/ppermute | solution.py:31
  51.5 11.0 %collective-permute-start.2 = (bf16[4,32,2048]{2,1,0:T(8,128)(2,1)S(1)}, bf16[4,32,2048]{2,1,0:T(8,128)(2,1)S(1)}, u32[]{:S(2)}, u32[]{:S(2)}) collective-permute-start(bf16[4,32,2048]{2,1,0:T(8,128)(2,1)S(1)} %get-tuple-element.40), channel_id=1, source_target_pairs={{0,3},{1,0},{2,1},{3,2},{4,7},{5,4},{6,5},{7,6},{8,11},{9,8},{10,9... | collective-permute-start | bytes 1572872 | tf_op jit(solution)/shard_map/ppermute | solution.py:31
  62.6 22.5 %collective-permute-done.1.e2 = bf16[4,32,2048]{2,1,0:T(8,128)(2,1)S(1)} collective-permute-done((bf16[4,32,2048]{2,1,0:T(8,128)(2,1)S(1)}, bf16[4,32,2048]{2,1,0:T(8,128)(2,1)S(1)}, u32[]{:S(2)}, u32[]{:S(2)}) %collective-permute-start.1) | collective-permute-done | bytes 524320 | tf_op jit(solution)/shard_map/ppermute | solution.py:31
  86.9 2.4 %forward.1.a0 = bf16[128,2048]{1,0:T(8,128)(2,1)S(1)} custom-call(s32[5]{0:T(128)S(1)} %stack.23.pos_ref, bf16[4,32,2048]{2,1,0:T(8,128)(2,1)S(1)} %get-tuple-element.33.e0, bf16[4,32,2048]{2,1,0:T(8,128)(2,1)S(1)} %collective-permute-done.e1, bf16[4,32,2048]{2,1,0:T(8,128)(2,1)S(1)} %collective-permute-done.1.e2, ...), custom_call_target="tpu_custom_call" | custom-call | tf_op jit(solution)/shard_map/forward/pallas_call | solution.py:184
  89.4 3.5 %collective-permute-start.3 = (bf16[128,2048]{1,0:T(8,128)(2,1)S(1)}, bf16[128,2048]{1,0:T(8,128)(2,1)S(1)}, u32[]{:S(2)}, u32[]{:S(2)}) collective-permute-start(bf16[128,2048]{1,0:T(8,128)(2,1)S(1)} %forward.1.a0), channel_id=1, source_target_pairs={{0,2},{1,3},{2,0},{3,1},{4,6},{5,7},{6,4},{7,5},{8,10},{9,11},{10,... | collective-permute-start | bytes 1572872 | tf_op jit(solution)/shard_map/ppermute | solution.py:31
  92.9 21.4 %collective-permute-done.3.a2 = bf16[128,2048]{1,0:T(8,128)(2,1)S(1)} collective-permute-done((bf16[128,2048]{1,0:T(8,128)(2,1)S(1)}, bf16[128,2048]{1,0:T(8,128)(2,1)S(1)}, u32[]{:S(2)}, u32[]{:S(2)}) %collective-permute-start.3) | collective-permute-done | bytes 524320 | tf_op jit(solution)/shard_map/ppermute | solution.py:31
  117.8 3.5 %collective-permute-start.5 = (bf16[128,2048]{1,0:T(8,128)(2,1)S(1)}, bf16[128,2048]{1,0:T(8,128)(2,1)S(1)}, u32[]{:S(2)}, u32[]{:S(2)}) collective-permute-start(bf16[128,2048]{1,0:T(8,128)(2,1)S(1)} %forward.1.a0), channel_id=1, source_target_pairs={{0,1},{1,2},{2,3},{3,0},{4,5},{5,6},{6,7},{7,4},{8,9},{9,10},{10,1... | collective-permute-start | bytes 1572872 | tf_op jit(solution)/shard_map/ppermute | solution.py:31
  129.5 8.5 %backward.1 = (bf16[3,32,2048]{2,1,0:T(8,128)(2,1)S(1)}, bf16[3,32,2048]{2,1,0:T(8,128)(2,1)S(1)}, bf16[3,32,2048]{2,1,0:T(8,128)(2,1)S(1)}, bf16[3,32,2048]{2,1,0:T(8,128)(2,1)}) custom-call(s32[5]{0:T(128)S(1)} %stack.23.pos_ref, bf16[4,32,2048]{2,1,0:T(8,128)(2,1)S(1)} %get-tuple-element.33.e0, bf16[4,32,2048]{2,1,0:T(8,128)(2,1)S(1)} %collective-permute-done.e1, ...), custom_call_target="tpu_custom_call" | custom-call | tf_op jit(solution)/shard_map/backward/pallas_call | solution.py:184
  138.0 8.1 %collective-permute-done.6.a3 = bf16[128,2048]{1,0:T(8,128)(2,1)S(1)} collective-permute-done((bf16[128,2048]{1,0:T(8,128)(2,1)S(1)}, bf16[128,2048]{1,0:T(8,128)(2,1)S(1)}, u32[]{:S(2)}, u32[]{:S(2)}) %collective-permute-start.6) | collective-permute-done | bytes 524320 | tf_op jit(solution)/shard_map/ppermute | solution.py:31
  146.1 3.0 %weight.1 = (f32[4,4,4,16,512]{4,3,2,1,0:T(8,128)S(1)}, f32[4,4,4,16,512]{4,3,2,1,0:T(8,128)S(1)}) custom-call(s32[5]{0:T(128)S(1)} %stack.23.pos_ref, bf16[128,2048]{1,0:T(8,128)(2,1)S(1)} %forward.1.a0, bf16[128,2048]{1,0:T(8,128)(2,1)S(1)} %collective-permute-done.5.a1, bf16[128,2048]{1,0:T(8,128)(2,1)S(1)} %collective-permute-done.3.a2, ...), custom_call_target="tpu_custom_call" | custom-call | tf_op jit(solution)/shard_map/weight/pallas_call | solution.py:184
  151.1 4.1 %collective-permute-done.7 = f32[4,4,4,16,512]{4,3,2,1,0:T(8,128)S(1)} collective-permute-done((f32[4,4,4,16,512]{4,3,2,1,0:T(8,128)S(1)}, f32[4,4,4,16,512]{4,3,2,1,0:T(8,128)S(1)}, u32[]{:S(2)}, u32[]{:S(2)}) %collective-permute-start.7) | collective-permute-done | bytes 2097184 | tf_op jit(solution)/shard_map/ppermute | solution.py:248
  157.3 6.3 %all-to-all-start.1 = ((f32[16,4,16,512]{3,2,1,0:T(8,128)}), f32[16,4,16,512]{3,2,1,0:T(8,128)}, u32[]{:S(2)}, u32[]{:S(2)}) async-start(f32[16,4,16,512]{3,2,1,0:T(8,128)} %bitcast.11), calls=%async_computation.1 | async-start | bytes 4194304 | tf_op jit(solution)/shard_map/all_to_all | solution.py:249
  163.6 3.4 %collective-permute-start.10 = (bf16[3,32,2048]{2,1,0:T(8,128)(2,1)}, bf16[3,32,2048]{2,1,0:T(8,128)(2,1)S(1)}, u32[]{:S(2)}, u32[]{:S(2)}) collective-permute-start(bf16[3,32,2048]{2,1,0:T(8,128)(2,1)} %get-tuple-element.56), channel_id=1, source_target_pairs={{0,3},{1,0},{2,1},{3,2},{4,7},{5,4},{6,5},{7,6},{8,11},{9,8},{10,9... | collective-permute-start | bytes 1179656 | tf_op jit(solution)/shard_map/ppermute | solution.py:31
  167.0 2.5 %collective-permute-start.8 = (bf16[3,32,2048]{2,1,0:T(8,128)(2,1)}, bf16[3,32,2048]{2,1,0:T(8,128)(2,1)S(1)}, u32[]{:S(2)}, u32[]{:S(2)}) collective-permute-start(bf16[3,32,2048]{2,1,0:T(8,128)(2,1)} %copy-done.15), channel_id=1, source_target_pairs={{0,1},{1,2},{2,3},{3,0},{4,5},{5,6},{6,7},{7,4},{8,9},{9,10},{10,1... | collective-permute-start | bytes 1179656 | tf_op jit(solution)/shard_map/ppermute | solution.py:31
  169.5 5.4 %collective-permute-start.9 = (bf16[3,32,2048]{2,1,0:T(8,128)(2,1)}, bf16[3,32,2048]{2,1,0:T(8,128)(2,1)}, u32[]{:S(2)}, u32[]{:S(2)}) collective-permute-start(bf16[3,32,2048]{2,1,0:T(8,128)(2,1)} %copy-done.14), channel_id=1, source_target_pairs={{0,2},{1,3},{2,0},{3,1},{4,6},{5,7},{6,4},{7,5},{8,10},{9,11},{10,... | collective-permute-start | bytes 1179656 | tf_op jit(solution)/shard_map/ppermute | solution.py:31
  179.3 3.1 %project.1 = bf16[16,32,512]{2,1,0:T(8,128)(2,1)} custom-call(s32[5]{0:T(128)S(1)} %stack.23.pos_ref, bf16[128,2048]{1,0:T(8,128)(2,1)S(1)} %forward.1.a0, bf16[128,2048]{1,0:T(8,128)(2,1)S(1)} %collective-permute-done.5.a1, bf16[128,2048]{1,0:T(8,128)(2,1)S(1)} %collective-permute-done.3.a2, bf16[128,2048]{1,0:T(8,128)(2,1)S(1)} %collective-permute-done.6.a3, ...), custom_call_target="tpu_custom_call" | custom-call | tf_op jit(solution)/shard_map/project/pallas_call | solution.py:184
  182.3 12.5 %all-to-all-done.1 = f32[16,4,16,512]{3,2,1,0:T(8,128)} async-done(((f32[16,4,16,512]{3,2,1,0:T(8,128)}), f32[16,4,16,512]{3,2,1,0:T(8,128)}, u32[]{:S(2)}, u32[]{:S(2)}) %all-to-all-start.1) | async-done | bytes 2097184 | tf_op jit(solution)/shard_map/all_to_all | solution.py:249
  197.2 11.1 %all-to-all-start.2 = ((f32[4,16,512]{2,1,0:T(8,128)}), f32[4,16,512]{2,1,0:T(8,128)S(1)}, u32[]{:S(2)}, u32[]{:S(2)}) async-start(f32[4,16,512]{2,1,0:T(8,128)} %reduce_sum.18), calls=%async_computation.2 | async-start | bytes 262144 | tf_op jit(solution)/shard_map/all_to_all | solution.py:267
  208.4 3.4 %unpack.1 = (bf16[4,32,2048]{2,1,0:T(8,128)(2,1)}, bf16[4,32,2048]{2,1,0:T(8,128)(2,1)}, bf16[4,32,2048]{2,1,0:T(8,128)(2,1)}) custom-call(s32[5]{0:T(128)S(1)} %stack.23.pos_ref, bf16[3,32,2048]{2,1,0:T(8,128)(2,1)S(1)} %get-tuple-element.53.h0, bf16[3,32,2048]{2,1,0:T(8,128)(2,1)S(1)} %collective-permute-done.8.h1, ...), custom_call_target="tpu_custom_call" | custom-call | tf_op jit(solution)/shard_map/unpack/pallas_call | solution.py:184
  211.8 10.7 %all-to-all-done.2 = f32[4,16,512]{2,1,0:T(8,128)S(1)} async-done(((f32[4,16,512]{2,1,0:T(8,128)}), f32[4,16,512]{2,1,0:T(8,128)S(1)}, u32[]{:S(2)}, u32[]{:S(2)}) %all-to-all-start.2) | async-done | bytes 131104 | tf_op jit(solution)/shard_map/all_to_all | solution.py:267
  (52 shorter events, 32.8 us)
Async XLA Ops:
  8.6 35.0 %all-to-all-start = ((bf16[16,16,512]{2,1,0:T(8,128)(2,1)}), bf16[16,16,512]{2,1,0:T(8,128)(2,1)S(1)}, u32[]{:S(2)}, u32[]{:S(2)}) async-start(bf16[16,16,512]{2,1,0:T(8,128)(2,1)} %broadcast_in_dim.2), calls=%async_computation | async-start | bytes 524288 | tf_op jit(solution)/shard_map/all_to_all | solution.py:201
  23.8 92.1 %all-gather.2.cloned.1.call-start = ((), (), s32[]{:S(2)}) async-start(), calls=%async_computation.3 | async-start | bytes 4456448 | tf_op jit(solution)/shard_map/all_gather | solution.py:212
  30.3 17.6 %collective-permute-start = (bf16[4,32,2048]{2,1,0:T(8,128)(2,1)S(1)}, bf16[4,32,2048]{2,1,0:T(8,128)(2,1)S(1)}, u32[]{:S(2)}, u32[]{:S(2)}) collective-permute-start(bf16[4,32,2048]{2,1,0:T(8,128)(2,1)S(1)} %get-tuple-element.37), channel_id=1, source_target_pairs={{0,1},{1,2},{2,3},{3,0},{4,5},{5,6},{6,7},{7,4},{8,9},{9,10},{10,1... | collective-permute-start | bytes 1572872 | tf_op jit(solution)/shard_map/ppermute | solution.py:31
  43.7 4.2 %copy-start.16 = (bf16[16,16,512]{2,1,0:T(8,128)(2,1)}, bf16[16,16,512]{2,1,0:T(8,128)(2,1)S(1)}, u32[]{:S(2)}) copy-start(bf16[16,16,512]{2,1,0:T(8,128)(2,1)S(1)} %all-to-all-done) | copy-start | bytes 786436
  47.9 37.2 %collective-permute-start.1 = (bf16[4,32,2048]{2,1,0:T(8,128)(2,1)S(1)}, bf16[4,32,2048]{2,1,0:T(8,128)(2,1)S(1)}, u32[]{:S(2)}, u32[]{:S(2)}) collective-permute-start(bf16[4,32,2048]{2,1,0:T(8,128)(2,1)S(1)} %get-tuple-element.39), channel_id=1, source_target_pairs={{0,2},{1,3},{2,0},{3,1},{4,6},{5,7},{6,4},{7,5},{8,10},{9,11},{10,... | collective-permute-start | bytes 1572872 | tf_op jit(solution)/shard_map/ppermute | solution.py:31
  51.5 35.4 %collective-permute-start.2 = (bf16[4,32,2048]{2,1,0:T(8,128)(2,1)S(1)}, bf16[4,32,2048]{2,1,0:T(8,128)(2,1)S(1)}, u32[]{:S(2)}, u32[]{:S(2)}) collective-permute-start(bf16[4,32,2048]{2,1,0:T(8,128)(2,1)S(1)} %get-tuple-element.40), channel_id=1, source_target_pairs={{0,3},{1,0},{2,1},{3,2},{4,7},{5,4},{6,5},{7,6},{8,11},{9,8},{10,9... | collective-permute-start | bytes 1572872 | tf_op jit(solution)/shard_map/ppermute | solution.py:31
  85.1 4.2 %copy-start.4 = (bf16[4,32,2048]{2,1,0:T(8,128)(2,1)}, bf16[4,32,2048]{2,1,0:T(8,128)(2,1)S(1)}, u32[]{:S(2)}) copy-start(bf16[4,32,2048]{2,1,0:T(8,128)(2,1)S(1)} %collective-permute-done.1.e2) | copy-start | bytes 1572868
  86.9 6.0 %copy-start.6 = (bf16[4,32,2048]{2,1,0:T(8,128)(2,1)}, bf16[4,32,2048]{2,1,0:T(8,128)(2,1)S(1)}, u32[]{:S(2)}) copy-start(bf16[4,32,2048]{2,1,0:T(8,128)(2,1)S(1)} %collective-permute-done.2.e3) | copy-start | bytes 1572868
  89.4 24.9 %collective-permute-start.3 = (bf16[128,2048]{1,0:T(8,128)(2,1)S(1)}, bf16[128,2048]{1,0:T(8,128)(2,1)S(1)}, u32[]{:S(2)}, u32[]{:S(2)}) collective-permute-start(bf16[128,2048]{1,0:T(8,128)(2,1)S(1)} %forward.1.a0), channel_id=1, source_target_pairs={{0,2},{1,3},{2,0},{3,1},{4,6},{5,7},{6,4},{7,5},{8,10},{9,11},{10,... | collective-permute-start | bytes 1572872 | tf_op jit(solution)/shard_map/ppermute | solution.py:31
  115.9 9.3 %collective-permute-start.4 = (bf16[4,4,4,4,16,512]{5,4,3,2,1,0:T(8,128)(2,1)}, bf16[4,4,4,4,16,512]{5,4,3,2,1,0:T(8,128)(2,1)S(1)}, u32[]{:S(2)}, u32[]{:S(2)}) collective-permute-start(bf16[4,4,4,4,16,512]{5,4,3,2,1,0:T(8,128)(2,1)} %bitcast.8), channel_id=1, source_target_pairs={{0,4},{4,0},{1,5},{5,1},{2,6},{6,2},{3,7},{7,3},{8,12},{12,8},{9,1... | collective-permute-start | bytes 12582920 | tf_op jit(solution)/shard_map/ppermute | solution.py:220
  117.8 20.2 %collective-permute-start.5 = (bf16[128,2048]{1,0:T(8,128)(2,1)S(1)}, bf16[128,2048]{1,0:T(8,128)(2,1)S(1)}, u32[]{:S(2)}, u32[]{:S(2)}) collective-permute-start(bf16[128,2048]{1,0:T(8,128)(2,1)S(1)} %forward.1.a0), channel_id=1, source_target_pairs={{0,1},{1,2},{2,3},{3,0},{4,5},{5,6},{6,7},{7,4},{8,9},{9,10},{10,1... | collective-permute-start | bytes 1572872 | tf_op jit(solution)/shard_map/ppermute | solution.py:31
  121.3 24.8 %collective-permute-start.6 = (bf16[128,2048]{1,0:T(8,128)(2,1)S(1)}, bf16[128,2048]{1,0:T(8,128)(2,1)S(1)}, u32[]{:S(2)}, u32[]{:S(2)}) collective-permute-start(bf16[128,2048]{1,0:T(8,128)(2,1)S(1)} %forward.1.a0), channel_id=1, source_target_pairs={{0,3},{1,0},{2,1},{3,2},{4,7},{5,4},{6,5},{7,6},{8,11},{9,8},{10,9... | collective-permute-start | bytes 1572872 | tf_op jit(solution)/shard_map/ppermute | solution.py:31
  125.2 2.2 copy-start
  129.5 8.5 %copy-start.2 = (bf16[4,4,4,4,16,512]{5,4,3,2,1,0:T(8,128)(2,1)}, bf16[4,4,4,4,16,512]{5,4,3,2,1,0:T(8,128)(2,1)S(1)}, u32[]{:S(2)}) copy-start(bf16[4,4,4,4,16,512]{5,4,3,2,1,0:T(8,128)(2,1)S(1)} %collective-permute-done.4.other_ref) | copy-start | bytes 12582916
  129.5 16.7 %copy-start.13 = (bf16[4,4,32,512]{3,2,1,0:T(8,128)(2,1)S(1)}, bf16[4,4,32,512]{3,2,1,0:T(8,128)(2,1)}, u32[]{:S(2)}) copy-start(bf16[4,4,32,512]{3,2,1,0:T(8,128)(2,1)} %copy-done.12) | copy-start | bytes 1572868
  138.0 19.3 %copy-start.14 = (bf16[3,32,2048]{2,1,0:T(8,128)(2,1)}, bf16[3,32,2048]{2,1,0:T(8,128)(2,1)S(1)}, u32[]{:S(2)}) copy-start(bf16[3,32,2048]{2,1,0:T(8,128)(2,1)S(1)} %get-tuple-element.55) | copy-start | bytes 1179652
  138.0 19.3 %copy-start.15 = (bf16[3,32,2048]{2,1,0:T(8,128)(2,1)}, bf16[3,32,2048]{2,1,0:T(8,128)(2,1)S(1)}, u32[]{:S(2)}) copy-start(bf16[3,32,2048]{2,1,0:T(8,128)(2,1)S(1)} %get-tuple-element.54) | copy-start | bytes 1179652
  149.1 6.1 %collective-permute-start.7 = (f32[4,4,4,16,512]{4,3,2,1,0:T(8,128)S(1)}, f32[4,4,4,16,512]{4,3,2,1,0:T(8,128)S(1)}, u32[]{:S(2)}, u32[]{:S(2)}) collective-permute-start(f32[4,4,4,16,512]{4,3,2,1,0:T(8,128)S(1)} %get-tuple-element.51), channel_id=1, source_target_pairs={{0,4},{4,0},{1,5},{5,1},{2,6},{6,2},{3,7},{7,3},{8,12},{12,8},{9,1... | collective-permute-start | bytes 6291464 | tf_op jit(solution)/shard_map/ppermute | solution.py:248
  157.3 37.6 %all-to-all-start.1 = ((f32[16,4,16,512]{3,2,1,0:T(8,128)}), f32[16,4,16,512]{3,2,1,0:T(8,128)}, u32[]{:S(2)}, u32[]{:S(2)}) async-start(f32[16,4,16,512]{3,2,1,0:T(8,128)} %bitcast.11), calls=%async_computation.1 | async-start | bytes 4194304 | tf_op jit(solution)/shard_map/all_to_all | solution.py:249
  163.6 44.8 %collective-permute-start.10 = (bf16[3,32,2048]{2,1,0:T(8,128)(2,1)}, bf16[3,32,2048]{2,1,0:T(8,128)(2,1)S(1)}, u32[]{:S(2)}, u32[]{:S(2)}) collective-permute-start(bf16[3,32,2048]{2,1,0:T(8,128)(2,1)} %get-tuple-element.56), channel_id=1, source_target_pairs={{0,3},{1,0},{2,1},{3,2},{4,7},{5,4},{6,5},{7,6},{8,11},{9,8},{10,9... | collective-permute-start | bytes 1179656 | tf_op jit(solution)/shard_map/ppermute | solution.py:31
  167.0 41.4 %collective-permute-start.8 = (bf16[3,32,2048]{2,1,0:T(8,128)(2,1)}, bf16[3,32,2048]{2,1,0:T(8,128)(2,1)S(1)}, u32[]{:S(2)}, u32[]{:S(2)}) collective-permute-start(bf16[3,32,2048]{2,1,0:T(8,128)(2,1)} %copy-done.15), channel_id=1, source_target_pairs={{0,1},{1,2},{2,3},{3,0},{4,5},{5,6},{6,7},{7,4},{8,9},{9,10},{10,1... | collective-permute-start | bytes 1179656 | tf_op jit(solution)/shard_map/ppermute | solution.py:31
  169.5 38.9 %collective-permute-start.9 = (bf16[3,32,2048]{2,1,0:T(8,128)(2,1)}, bf16[3,32,2048]{2,1,0:T(8,128)(2,1)}, u32[]{:S(2)}, u32[]{:S(2)}) collective-permute-start(bf16[3,32,2048]{2,1,0:T(8,128)(2,1)} %copy-done.14), channel_id=1, source_target_pairs={{0,2},{1,3},{2,0},{3,1},{4,6},{5,7},{6,4},{7,5},{8,10},{9,11},{10,... | collective-permute-start | bytes 1179656 | tf_op jit(solution)/shard_map/ppermute | solution.py:31
  174.9 2.2 copy-start.1
  197.2 25.2 %all-to-all-start.2 = ((f32[4,16,512]{2,1,0:T(8,128)}), f32[4,16,512]{2,1,0:T(8,128)S(1)}, u32[]{:S(2)}, u32[]{:S(2)}) async-start(f32[4,16,512]{2,1,0:T(8,128)} %reduce_sum.18), calls=%async_computation.2 | async-start | bytes 262144 | tf_op jit(solution)/shard_map/all_to_all | solution.py:267
  (8 other events, 9.2 us)
Sparse Core Ops, SparseCore 0:
  48.0 67.8 all-gather.1
